TPU v7x, 32 devices: a whole 2x2x4 slice. The times are simulated.
32 devices in a mesh: row: 4 (over y, x), col: 8 (over z, core).
Axes of the slice: x: 2, y: 2, z: 4, core: 2. Of those that a mesh axis runs over, the one named last changes fastest.
Arguments:
- patches: bfloat16 [192, 196, 768], P(('row', 'col')), may hold values from -6 to 6
- shuffle: int32 [192, 196], P(('row', 'col')), may hold values from 0 to 195, each once within a row
- enc_w: float32 [768, 3840], P('row', 'col'), may hold values from -0.21875 to 0.21875
- enc_ffn: float32 [2, 768, 3072], P(None, 'row', 'col'), may hold values from -0.21875 to 0.21875
- dec_proj: float32 [768, 512], P('row', 'col'), may hold values from -0.21875 to 0.21875
- dec_w: float32 [512, 2048], P('row', 'col'), may hold values from -0.25 to 0.25
- dec_ffn: float32 [2, 512, 2048], P(None, 'row', 'col'), may hold values from -0.25 to 0.25
- head_w: float32 [512, 768], replicated, may hold values from -0.25 to 0.25
- smalls: float32 [21248], replicated, may hold values from 0.5 to 1.5
- first_enc_w: float32 [768, 3840], P('row', 'col'), may hold values from -0.00012207031 to 0.00012207031
- first_enc_ffn: float32 [2, 768, 3072], P(None, 'row', 'col'), may hold values from -0.00012207031 to 0.00012207031
- first_dec_proj: float32 [768, 512], P('row', 'col'), may hold values from -0.00012207031 to 0.00012207031
- first_dec_w: float32 [512, 2048], P('row', 'col'), may hold values from -0.00012207031 to 0.00012207031
- first_dec_ffn: float32 [2, 512, 2048], P(None, 'row', 'col'), may hold values from -0.00012207031 to 0.00012207031
- first_head_w: float32 [512, 768], replicated, may hold values from -0.00012207031 to 0.00012207031
- first_smalls: float32 [21248], replicated, may hold values from -0.0014648438 to 0.0014648438
- second_enc_w: float32 [768, 3840], P('row', 'col'), may hold values from 5.406317e-10 to 2.1625268e-09
- second_enc_ffn: float32 [2, 768, 3072], P(None, 'row', 'col'), may hold values from 5.406317e-10 to 2.1625268e-09
- second_dec_proj: float32 [768, 512], P('row', 'col'), may hold values from 5.406317e-10 to 2.1625268e-09
- second_dec_w: float32 [512, 2048], P('row', 'col'), may hold values from 5.406317e-10 to 2.1625268e-09
- second_dec_ffn: float32 [2, 512, 2048], P(None, 'row', 'col'), may hold values from 5.406317e-10 to 2.1625268e-09
- second_head_w: float32 [512, 768], replicated, may hold values from 5.406317e-10 to 2.1625268e-09
- second_smalls: float32 [21248], replicated, may hold values from 5.4063168e-08 to 2.1625267e-07
Outputs:
- new_enc_w: float32 [768, 3840], P('row', 'col')
- new_enc_ffn: float32 [2, 768, 3072], P(None, 'row', 'col')
- new_dec_proj: float32 [768, 512], P('row', 'col')
- new_dec_w: float32 [512, 2048], P('row', 'col')
- new_dec_ffn: float32 [2, 512, 2048], P(None, 'row', 'col')
- new_head_w: float32 [512, 768], replicated
- new_smalls: float32 [21248], replicated
- moment_enc_w: float32 [768, 3840], P('row', 'col')
- moment_enc_ffn: float32 [2, 768, 3072], P(None, 'row', 'col')
- moment_dec_proj: float32 [768, 512], P('row', 'col')
- moment_dec_w: float32 [512, 2048], P('row', 'col')
- moment_dec_ffn: float32 [2, 512, 2048], P(None, 'row', 'col')
- moment_head_w: float32 [512, 768], replicated
- moment_smalls: float32 [21248], replicated
- square_enc_w: float32 [768, 3840], P('row', 'col')
- square_enc_ffn: float32 [2, 768, 3072], P(None, 'row', 'col')
- square_dec_proj: float32 [768, 512], P('row', 'col')
- square_dec_w: float32 [512, 2048], P('row', 'col')
- square_dec_ffn: float32 [2, 512, 2048], P(None, 'row', 'col')
- square_head_w: float32 [512, 768], replicated
- square_smalls: float32 [21248], replicated
- loss: float32 [], replicated
Inputs may be any that keep to these rules, and one draw needn't show every extreme that they name: `shuffle`: each image's row names every patch index once.
All inputs are finite; a program needn't handle non-finite values.
Results may differ from a plain program's by a relative error of at most 0.00095.
The roundings to bfloat16 on the way count: a program that leaves them out, or rounds other values in their place, can miss the bound.
Values may be sent and summed in bfloat16 or wider, within the bound.
A program may use at most 256 MiB of HBM per device.

v0:
```python
import functools
import math

import jax
import jax.numpy as jnp
import numpy as np
from jax import lax
from jax.experimental import pallas as pl
from jax.experimental.pallas import tpu as pltpu
from jax.sharding import PartitionSpec as P

D = 768
HE = 12
F = 3072
E = 512
HD = 16
H = 2048
P_SIZE = 768
SIDE = 14
KEEP = 49
STEP = 5
PATCHES = 196
LANES = 128

norm_eps = 1e-06
low_type = jnp.bfloat16
high_type = jnp.float32


def unpack(smalls):
    first = 12 * D
    second = first + F
    third = second + 12 * E
    fourth = third + H
    return (
        smalls[:first].reshape(12, D),
        smalls[first:second],
        smalls[second:third].reshape(12, E),
        smalls[third:fourth],
        smalls[fourth:],
    )


MESH = pl.DeviceIdType.MESH


class Group:
    def __init__(self, copies):
        self.copies = copies

    def start(self):
        for item in self.copies:
            item.start()

    def wait_recv(self):
        for item in self.copies:
            item.wait_recv()

    def wait_send(self):
        for item in self.copies:
            item.wait_send()

    def wait(self):
        for item in self.copies:
            item.wait()


def gather_kernel(depth, own_enc, own_ffn, own_proj, own_dec, enc, ffn, proj, dec,
                  zs, zr, xs, xr, ys, yr, dxs, dxr, dys, dyr, cs, cr, local):
    row = lax.axis_index("row")
    col = lax.axis_index("col")
    y, x, z, k = row // 2, row % 2, col // 2, col % 2
    row_x = y * 2 + (1 - x)
    row_y = (1 - y) * 2 + x
    row_d = (1 - y) * 2 + (1 - x)
    near_x, near_y = (row_x, col), (row_y, col)
    twin = (row, z * 2 + (1 - k))
    lower, upper = (row, col - 2), (row, col + 2)
    has_lower, has_upper = z > 0, z < depth - 1
    own = (own_enc, own_ffn, own_proj, own_dec)

    barrier = pltpu.get_barrier_semaphore()
    for other in (near_x, near_y, twin):
        pl.semaphore_signal(barrier, inc=1, device_id=other, device_id_type=MESH)

    @pl.when(has_lower)
    def _():
        pl.semaphore_signal(barrier, inc=1, device_id=lower, device_id_type=MESH)

    @pl.when(has_upper)
    def _():
        pl.semaphore_signal(barrier, inc=1, device_id=upper, device_id_type=MESH)

    pl.semaphore_wait(barrier, 3 + jnp.where(has_lower, 1, 0) + jnp.where(has_upper, 1, 0))

    levels = [(0, 0)] + [(d, way) for d in range(1, depth) for way in (0, 1)]
    level_of = {item: number for number, item in enumerate(levels)}

    def place(level):
        d, way = level
        return z - d if way == 0 else z + d

    def valid(level):
        d, way = level
        return z - d >= 0 if way == 0 else z + d < depth

    def cut(index, row_now, half=None):
        def rows(size, unit):
            part = size if half is None else size // 2
            first = 0 if half is None else half * part
            return pl.ds(pl.multiple_of(row_now * size + first, 16), part)

        tall, short = own_enc.shape[0], own_dec.shape[1]
        wide, thin = own_ffn.shape[2], own_dec.shape[2]
        return (
            enc.at[index, rows(tall, 16)],
            ffn.at[:, rows(tall, 16), pl.ds(pl.multiple_of(index * wide, LANES), wide)],
            proj.at[index, rows(tall, 16)],
            dec.at[:, rows(short, 16), pl.ds(pl.multiple_of(index * thin, LANES), thin)],
        )

    def slot(level, row_now, half=None):
        return cut(place(level) * 2 + k, row_now, half)

    def source(level):
        return own if level == (0, 0) else slot(level, row)

    def copy(src, dst, send, recv, target):
        return Group(
            [
                pltpu.make_async_remote_copy(
                    src_ref=src[item],
                    dst_ref=dst[item],
                    send_sem=send.at[item],
                    recv_sem=recv.at[item],
                    device_id=target,
                    device_id_type=MESH,
                )
                for item in range(4)
            ]
        )

    def z_copy(level, way):
        d = level[0]
        n = level_of[level]
        return copy(source(level), slot(level, row), zs.at[n, way], zr.at[d, way], upper if way == 0 else lower)

    def x_copy(level):
        n = level_of[level]
        return copy(source(level), slot(level, row), xs.at[n], xr.at[n], near_x)

    def y_copy(level):
        n = level_of[level]
        return copy(source(level), slot(level, row), ys.at[n], yr.at[n], near_y)

    def dx_copy(level):
        n = level_of[level]
        refs = slot(level, row_y, 1)
        return copy(refs, refs, dxs.at[n], dxr.at[n], near_x)

    def dy_copy(level):
        n = level_of[level]
        refs = slot(level, row_x, 0)
        return copy(refs, refs, dys.at[n], dyr.at[n], near_y)

    def twin_copy(level, kind):
        n = level_of[level]
        row_now = (row, row_x, row_y, row_d)[kind]
        src = source(level) if kind == 0 else slot(level, row_now)
        return copy(src, slot(level, row_now), cs.at[n, kind], cr.at[n, kind], twin)

    def guarded(level, action):
        if level == (0, 0):
            action()
        else:
            pl.when(valid(level))(action)

    def spread(level):
        d, way = level

        def action():
            if level != (0, 0):
                z_copy((d - 1, way if d > 1 else 0), way).wait_recv()
            for direction in (0, 1):
                if level == (0, 0) or direction == way:
                    @pl.when(has_upper if direction == 0 else has_lower)
                    def _():
                        z_copy(level, direction).start()
            x_copy(level).start()
            y_copy(level).start()
            twin_copy(level, 0).start()

        guarded(level, action)

    def turn(level):
        def action():
            x_copy(level).wait_recv()
            dy_copy(level).start()
            twin_copy(level, 1).start()
            y_copy(level).wait_recv()
            dx_copy(level).start()
            twin_copy(level, 2).start()

        guarded(level, action)

    def close(level):
        def action():
            dx_copy(level).wait_recv()
            dy_copy(level).wait_recv()
            twin_copy(level, 3).start()

        guarded(level, action)

    def drain(level):
        d, way = level

        def action():
            for direction in (0, 1):
                if level == (0, 0) or direction == way:
                    @pl.when(has_upper if direction == 0 else has_lower)
                    def _():
                        z_copy(level, direction).wait_send()
            x_copy(level).wait_send()
            y_copy(level).wait_send()
            dx_copy(level).wait_send()
            dy_copy(level).wait_send()
            for kind in range(4):
                twin_copy(level, kind).wait()

        guarded(level, action)

    keep = Group(
        [pltpu.make_async_copy(src, dst, local.at[item]) for item, (src, dst) in enumerate(zip(own, cut(col, row)))]
    )
    keep.start()
    for step in range(depth + 2):
        for level in levels:
            if level[0] == step:
                spread(level)
        for level in levels:
            if level[0] == step - 1:
                turn(level)
        for level in levels:
            if level[0] == step - 2:
                close(level)
    keep.wait()
    for level in levels:
        drain(level)


def gather_blocks(own_enc, own_ffn, own_proj, own_dec, depth):
    count = 2 * depth - 1
    cols = 2 * depth
    dma = pltpu.SemaphoreType.DMA
    anywhere = pl.BlockSpec(memory_space=pltpu.HBM)
    tall, width = own_enc.shape
    shape = jax.ShapeDtypeStruct
    kind = own_enc.dtype
    return pl.pallas_call(
        functools.partial(gather_kernel, depth),
        out_shape=(
            shape((cols, 4 * tall, width), kind),
            shape((2, 4 * tall, cols * own_ffn.shape[2]), kind),
            shape((cols, 4 * tall, own_proj.shape[1]), kind),
            shape((3, 4 * own_dec.shape[1], cols * own_dec.shape[2]), kind),
        ),
        in_specs=[anywhere] * 4,
        out_specs=[anywhere] * 4,
        scratch_shapes=[dma((count, 2, 4)), dma((depth, 2, 4))]
        + [dma((count, 4)) for _ in range(8)]
        + [dma((count, 4, 4)), dma((count, 4, 4)), dma((4,))],
        compiler_params=pltpu.CompilerParams(collective_id=0, has_side_effects=True),
        name="gather_blocks",
    )(own_enc, own_ffn, own_proj, own_dec)


def far_first(depth):
    orders = []
    for z in range(depth):
        orders.append(sorted(range(depth), key=lambda t: (-abs(t - z), -abs(2 * t - depth + 1))))
    return orders


code_type = jnp.int16
code_top = 32767.0


def encode(values):
    peak = jnp.max(jnp.abs(values), axis=0, keepdims=True)
    unit = jnp.maximum(peak, 1e-30) * (1.0 / code_top)
    codes = jnp.round(values * (1.0 / unit))
    codes = jnp.clip(codes, -code_top, code_top)
    return codes.astype(jnp.int32).astype(code_type), unit


def decode(codes, unit):
    return codes.astype(jnp.int32).astype(high_type) * unit


def reduce_kernel(depth, devices, cols, parts, chunk, half, blob, small, out, small_out,
                  arrived, mine, stage_x, stage_y, recv_x, recv_y, turn_x, turn_y, back_x, back_y, line_out, line,
                  units_out, units_in, line_units, box,
                  s_load, s_cs, s_cr, s_xs, s_xr, s_ys, s_yr, s_txs, s_txr, s_tys, s_tyr, s_zs, s_zr,
                  u_xs, u_xr, u_ys, u_yr, u_txs, u_txr, u_tys, u_tyr, u_zs, u_zr,
                  s_ps, s_pr, s_qs, s_qr):
    row = lax.axis_index("row")
    col = lax.axis_index("col")
    y, x, z, k = row // 2, row % 2, col // 2, col % 2
    me = row * cols + col
    near_x, near_y = (y * 2 + (1 - x), col), ((1 - y) * 2 + x, col)
    twin = (row, z * 2 + (1 - k))
    lower, upper = (row, col - 2), (row, col + 2)
    has_lower, has_upper = z > 0, z < depth - 1
    steps = depth * parts
    slots = mine.shape[0]
    ahead = slots - 1
    a_rows, b_rows = pl.ds(0, half), pl.ds(half, chunk - half)

    def device(offset):
        index = (me + offset) % devices
        return (index // cols, index % cols)

    barrier = pltpu.get_barrier_semaphore()
    for offset in range(1, devices):
        pl.semaphore_signal(barrier, inc=1, device_id=device(offset), device_id_type=MESH)
    pl.semaphore_wait(barrier, devices - 1)

    def copy(src, dst, send, recv, target):
        return pltpu.make_async_remote_copy(
            src_ref=src, dst_ref=dst, send_sem=send, recv_sem=recv, device_id=target, device_id_type=MESH
        )

    orders = far_first(depth)

    def goal(t):
        turn = t // parts
        value = 0
        for a in range(depth):
            for b in range(depth):
                value = jnp.where((z == a) & (turn == b), orders[a][b], value)
        return value

    def span(t):
        return pl.ds(pl.multiple_of((t % parts) * chunk, 16), chunk)

    def load(t):
        return pltpu.make_async_copy(
            blob.at[goal(t) * 2 + k, :, span(t)], mine.at[t % slots], s_load.at[t % slots]
        )

    def core(t):
        return copy(blob.at[goal(t) * 2 + (1 - k), :, span(t)], arrived.at[t], s_cs.at[t], s_cr.at[t], twin)

    def paired(kind, src, dst, send, recv, unit_send, unit_recv, target):
        def make(t):
            return Group([
                copy(src.at[t], dst.at[t], send.at[t], recv.at[t], target),
                copy(units_out.at[t, kind], units_in.at[t, kind], unit_send.at[t], unit_recv.at[t], target),
            ])

        return make

    first_x = paired(0, stage_x, recv_x, s_xs, s_xr, u_xs, u_xr, near_x)
    first_y = paired(1, stage_y, recv_y, s_ys, s_yr, u_ys, u_yr, near_y)
    second_x = paired(2, turn_x, back_x, s_txs, s_txr, u_txs, u_txr, near_x)
    second_y = paired(3, turn_y, back_y, s_tys, s_tyr, u_tys, u_tyr, near_y)

    def along(t, index, target):
        return Group([
            copy(line_out.at[t], line.at[index], s_zs.at[t], s_zr.at[index], target),
            copy(units_out.at[t, 4], line_units.at[index], u_zs.at[t], u_zr.at[index], target),
        ])

    def upper_index(t):
        return (goal(t) + 1) * parts + t % parts

    def lower_index(t):
        return goal(t) * parts + t % parts

    def to_upper(t):
        return along(t, upper_index(t), upper)

    def to_lower(t):
        return along(t, lower_index(t), lower)

    def small_send(offset):
        target = device(offset)
        return copy(small.at[target[0] * cols + target[1]], box.at[offset], s_ps.at[offset], s_pr.at[offset], target)

    def small_back(offset):
        return copy(small_out.at[me], small_out.at[me], s_qs.at[offset], s_qr.at[offset], device(offset))

    def small_back_recv(offset):
        origin = (me + devices - offset) % devices
        return copy(small_out.at[origin], small_out.at[origin], s_qs.at[offset], s_qr.at[offset], device(offset))

    for t in range(ahead):
        load(t).start()
        core(t).start()
    for offset in range(1, devices):
        small_send(offset).start()

    def stage_one(t):
        load(t).wait()
        core(t).wait_recv()
        slot = t % slots
        for other in (0, 1):
            away = other * 2 + (1 - x)
            stay = other * 2 + x
            codes, unit = encode(mine[slot, away, a_rows] + arrived[t, away, a_rows])
            stage_x[t, other] = codes
            units_out[t, 0, pl.ds(other, 1)] = unit
            arrived[t, stay, a_rows] += mine[slot, stay, a_rows]
        first_x(t).start()
        for other in (0, 1):
            away = (1 - y) * 2 + other
            stay = y * 2 + other
            codes, unit = encode(mine[slot, away, b_rows] + arrived[t, away, b_rows])
            stage_y[t, other] = codes
            units_out[t, 1, pl.ds(other, 1)] = unit
            arrived[t, stay, b_rows] += mine[slot, stay, b_rows]
        first_y(t).start()

    def stage_two(t):
        first_x(t).wait_recv()
        away = (1 - y) * 2 + x
        codes, unit = encode(arrived[t, away, a_rows] + decode(recv_x[t, 1 - y], units_in[t, 0, pl.ds(1 - y, 1)]))
        turn_y[t] = codes
        units_out[t, 3, pl.ds(0, 1)] = unit
        second_y(t).start()
        arrived[t, row, a_rows] += decode(recv_x[t, y], units_in[t, 0, pl.ds(y, 1)])
        first_y(t).wait_recv()
        away = y * 2 + (1 - x)
        codes, unit = encode(arrived[t, away, b_rows] + decode(recv_y[t, 1 - x], units_in[t, 1, pl.ds(1 - x, 1)]))
        turn_x[t] = codes
        units_out[t, 2, pl.ds(0, 1)] = unit
        second_x(t).start()
        arrived[t, row, b_rows] += decode(recv_y[t, x], units_in[t, 1, pl.ds(x, 1)])

    def stage_three(t):
        second_y(t).wait_recv()
        arrived[t, row, a_rows] += decode(back_y[t], units_in[t, 3, pl.ds(0, 1)])
        second_x(t).wait_recv()
        arrived[t, row, b_rows] += decode(back_x[t], units_in[t, 2, pl.ds(0, 1)])

    def take(index):
        return decode(line[index], line_units[index, pl.ds(0, 1)])

    def pack(t):
        codes, unit = encode(arrived[t, row])
        line_out[t] = codes
        units_out[t, 4, pl.ds(0, 1)] = unit

    def stage_four(t):
        target = goal(t)

        @pl.when((target >= z) & has_lower)
        def _():
            to_upper(t).wait_recv()
            arrived[t, row] += take(upper_index(t))

        @pl.when((target <= z) & has_upper)
        def _():
            to_lower(t).wait_recv()
            arrived[t, row] += take(lower_index(t))

        @pl.when(target != z)
        def _():
            pack(t)

        @pl.when(target > z)
        def _():
            to_upper(t).start()

        @pl.when(target < z)
        def _():
            to_lower(t).start()

        @pl.when(target == z)
        def _():
            out[span(t)] = arrived[t, row]

    lags = (2, 4, 6)

    def body(i, carry):
        @pl.when(i + ahead < steps)
        def _():
            load(i + ahead).start()
            core(i + ahead).start()

        @pl.when(i < steps)
        def _():
            stage_one(i)

        for lag, stage in zip(lags, (stage_two, stage_three, stage_four)):
            @pl.when((i >= lag) & (i - lag < steps))
            def _():
                stage(i - lag)

        @pl.when(i == steps // 2)
        def _():
            total = small[me]
            for offset in range(1, devices):
                small_send(offset).wait_recv()
                total = total + box[offset]
            small_out[me] = total
            for offset in range(1, devices):
                small_back(offset).start()

        return carry

    lax.fori_loop(0, steps + lags[-1], body, 0)

    def finish(t, carry):
        core(t).wait_send()
        first_x(t).wait_send()
        first_y(t).wait_send()
        second_x(t).wait_send()
        second_y(t).wait_send()

        @pl.when(goal(t) > z)
        def _():
            to_upper(t).wait_send()

        @pl.when(goal(t) < z)
        def _():
            to_lower(t).wait_send()

        return carry

    lax.fori_loop(0, steps, finish, 0)
    for offset in range(1, devices):
        small_send(offset).wait_send()
        small_back(offset).wait_send()
        small_back_recv(offset).wait_recv()


def reduce_blocks(blob, small, depth, parts):
    cols, _, rows, lanes = blob.shape
    devices = 4 * cols
    chunk = rows // parts
    half = -(-chunk // 32) * 16
    rest = chunk - half
    steps = depth * parts
    lines = (depth + 1) * parts
    dma = pltpu.SemaphoreType.DMA
    vm = pltpu.VMEM
    return pl.pallas_call(
        functools.partial(reduce_kernel, depth, devices, cols, parts, chunk, half),
        out_shape=(
            jax.ShapeDtypeStruct((rows, lanes), high_type),
            jax.ShapeDtypeStruct(small.shape, high_type),
        ),
        in_specs=[pl.BlockSpec(memory_space=pltpu.HBM), pl.BlockSpec(memory_space=pltpu.VMEM)],
        out_specs=[pl.BlockSpec(memory_space=pltpu.VMEM)] * 2,
        scratch_shapes=[
            vm((steps, 4, chunk, lanes), high_type),
            vm((4, 4, chunk, lanes), high_type),
            vm((steps, 2, half, lanes), code_type),
            vm((steps, 2, rest, lanes), code_type),
            vm((steps, 2, half, lanes), code_type),
            vm((steps, 2, rest, lanes), code_type),
            vm((steps, rest, lanes), code_type),
            vm((steps, half, lanes), code_type),
            vm((steps, rest, lanes), code_type),
            vm((steps, half, lanes), code_type),
            vm((steps, chunk, lanes), code_type),
            vm((lines, chunk, lanes), code_type),
            vm((steps, 5, 8, lanes), high_type),
            vm((steps, 4, 8, lanes), high_type),
            vm((lines, 8, lanes), high_type),
            vm((devices,) + small.shape[1:], high_type),
            dma((4,)),
        ]
        + ([dma((steps,)) for _ in range(11)] + [dma((lines,))])
        + ([dma((steps,)) for _ in range(9)] + [dma((lines,))])
        + [dma((devices,)) for _ in range(4)],
        compiler_params=pltpu.CompilerParams(
            collective_id=1, has_side_effects=True, vmem_limit_bytes=62 << 20
        ),
        name="reduce_blocks",
    )(blob, small)


ENC_ROWS = 64
DEC_ROWS = 208
CLASS_ENC = KEEP
CLASS_DEC = PATCHES
NEGATIVE = -1e30


def nn(left, right):
    return jnp.dot(left, right, preferred_element_type=high_type)


def nt(left, right):
    return lax.dot_general(left, right, (((1,), (1,)), ((), ())), preferred_element_type=high_type)


def tn(left, right):
    return lax.dot_general(left, right, (((0,), (0,)), ((), ())), preferred_element_type=high_type)


def standard(rows):
    mean = jnp.mean(rows, -1, keepdims=True)
    centred = rows - mean
    spread = jnp.mean(centred * centred, -1, keepdims=True)
    rate = lax.rsqrt(spread + norm_eps)
    return centred * rate, rate


def standard_back(unit, rate, grad):
    return rate * (grad - jnp.mean(grad, -1, keepdims=True) - unit * jnp.mean(grad * unit, -1, keepdims=True))


def col_sum(rows):
    return jnp.sum(rows.astype(high_type), 0, keepdims=True)


def gelu_pair(value):
    size = jnp.abs(value)
    below = 1.0 + (0.3275911 * math.sqrt(0.5)) * size
    t = pl.reciprocal(below, approx=True)
    t = t * (2.0 - below * t)
    t = t * (2.0 - below * t)
    fall = jnp.exp(-0.5 * value * value)
    series = 1.061405429
    for item in (-1.453152027, 1.421413741, -0.284496736, 0.254829592):
        series = series * t + item
    tail = 0.5 * series * t * fall
    part = jnp.where(value < 0.0, tail, 1.0 - tail)
    return value * part, part + value * fall * (1.0 / math.sqrt(2.0 * math.pi))


def three_way(value):
    high = value.astype(low_type)
    rest = value - high.astype(high_type)
    middle = rest.astype(low_type)
    return high, middle, (rest - middle.astype(high_type)).astype(low_type)


def place_rows(picks, value):
    parts = three_way(value)
    return nn(picks, parts[0]) + nn(picks, parts[1]) + nn(picks, parts[2])


def stack_heads(value, heads):
    width = LANES // heads
    lane = lax.broadcasted_iota(jnp.int32, value.shape, 1) // width
    return jnp.concatenate([jnp.where(lane == head, value, jnp.zeros_like(value)) for head in range(heads)], 0)


def merge_heads(stacked, heads):
    rows = stacked.shape[0] // heads
    width = LANES // heads
    lane = lax.broadcasted_iota(jnp.int32, (rows, LANES), 1) // width
    merged = stacked[:rows]
    for head in range(1, heads):
        merged = jnp.where(lane == head, stacked[head * rows : (head + 1) * rows], merged)
    return merged


def attend(query, key, value, heads, length):
    scores = nt(stack_heads(query, heads), key)
    column = lax.broadcasted_iota(jnp.int32, scores.shape, 1)
    scores = jnp.where(column < length, scores, NEGATIVE)
    raised = jnp.exp(scores - jnp.max(scores, -1, keepdims=True))
    attention = (raised / jnp.sum(raised, -1, keepdims=True)).astype(low_type)
    return merge_heads(nn(attention, value), heads)


def attend_back(query, key, value, grad, heads, length):
    queries = stack_heads(query, heads)
    grads = stack_heads(grad, heads)
    scores = nt(key, queries)
    place = lax.broadcasted_iota(jnp.int32, scores.shape, 0)
    scores = jnp.where(place < length, scores, NEGATIVE)
    raised = jnp.exp(scores - jnp.max(scores, 0, keepdims=True))
    attention = raised * (1.0 / jnp.sum(raised, 0, keepdims=True))
    inner = nt(value, grads)
    grad_scores = (attention * (inner - jnp.sum(inner * attention, 0, keepdims=True))).astype(low_type)
    grad_value = nn(attention.astype(low_type), grads)
    grad_key = nn(grad_scores, queries)
    grad_query = merge_heads(tn(grad_scores, key), heads)
    return grad_query, grad_key, grad_value


def attend_back_many(batch, query, key, value, grad, heads, length):
    rows = query.shape[0] // batch
    spans = [slice(image * rows, (image + 1) * rows) for image in range(batch)]
    queries = [stack_heads(query[span], heads) for span in spans]
    grads = [stack_heads(grad[span], heads) for span in spans]
    scores = jnp.concatenate([nt(key[span], item) for span, item in zip(spans, queries)], 0)
    inner = jnp.concatenate([nt(value[span], item) for span, item in zip(spans, grads)], 0)
    scores = scores.reshape(batch, rows, scores.shape[1])
    inner = inner.reshape(batch, rows, inner.shape[1])
    place = lax.broadcasted_iota(jnp.int32, scores.shape, 1)
    scores = jnp.where(place < length, scores, NEGATIVE)
    raised = jnp.exp(scores - jnp.max(scores, 1, keepdims=True))
    attention = raised * (1.0 / jnp.sum(raised, 1, keepdims=True))
    grad_scores = (attention * (inner - jnp.sum(inner * attention, 1, keepdims=True))).astype(low_type)
    attention = attention.astype(low_type)
    grad_value = [nn(attention[image], grads[image]) for image in range(batch)]
    grad_key = [nn(grad_scores[image], queries[image]) for image in range(batch)]
    grad_query = [merge_heads(tn(grad_scores[image], key[spans[image]]), heads) for image in range(batch)]
    return tuple(jnp.concatenate(item, 0) for item in (grad_query, grad_key, grad_value))


def wide_kernel(blocks, wide):
    count, _, width = blocks.shape
    for index in range(count):
        wide[:, index * width : (index + 1) * width] = blocks[index]


def enc_attend_kernel(batch, pick, patches, wide, vec, pos, kept, start, normed, qkv, mixed, middle, normed_two):
    rows = ENC_ROWS
    for image in range(batch):
        span = pl.ds(image * rows, rows)
        kept[span] = nn(pick[image], patches[image]).astype(low_type)
    start[...] = nn(kept[...], wide[:, :D]) + vec[0:1]
    parts = three_way(pos[...])
    for image in range(batch):
        span = pl.ds(image * rows, rows)
        picks = pick[image]
        placed = nn(picks, parts[0]) + nn(picks, parts[1]) + nn(picks, parts[2])
        inner = lax.broadcasted_iota(jnp.int32, placed.shape, 0)
        start[span] = jnp.where(inner == CLASS_ENC, vec[1:2], start[span] + placed)
    unit, _ = standard(start[...])
    normed[...] = (unit * vec[2:3] + vec[3:4]).astype(low_type)
    scale = 1.0 / math.sqrt(D // HE)
    rows_in = normed[...]
    qkv[:, :D] = ((nn(rows_in, wide[:, D : 2 * D]) + vec[4:5]) * scale).astype(low_type)
    qkv[:, D : 2 * D] = nn(rows_in, wide[:, 2 * D : 3 * D]).astype(low_type)
    qkv[:, 2 * D :] = (nn(rows_in, wide[:, 3 * D : 4 * D]) + vec[5:6]).astype(low_type)
    heads = LANES * HE // D
    for image in range(batch):
        span = pl.ds(image * rows, rows)
        for group in range(D // LANES):
            lane = group * LANES
            mixed[span, lane : lane + LANES] = attend(
                qkv[span, lane : lane + LANES],
                qkv[span, D + lane : D + lane + LANES],
                qkv[span, 2 * D + lane : 2 * D + lane + LANES],
                heads,
                KEEP + 1,
            ).astype(low_type)
    middle[...] = start[...] + (nn(mixed[...], wide[:, 4 * D :]) + vec[6:7])
    unit, _ = standard(middle[...])
    normed_two[...] = (unit * vec[7:8] + vec[8:9]).astype(low_type)


def enc_ffn_kernel(last, middle, normed_two, ffn, vec, up_bias, proj, dec_vec, slope, active, output, latent, entry):
    step = pl.program_id(0)

    @pl.when(step == 0)
    def _():
        output[...] = middle[...] + vec[9:10]

    value, gain = gelu_pair(nn(normed_two[...], ffn[0]) + up_bias[...])
    slope[...] = gain
    value = value.astype(low_type)
    active[...] = value
    output[...] += nt(value, ffn[1])

    @pl.when(step == last)
    def _():
        unit, _ = standard(output[...])
        rows = (unit * vec[10:11] + vec[11:12]).astype(low_type)
        latent[...] = rows
        entry[...] = nn(rows, proj[...]) + dec_vec[0:1]


def dec_attend_kernel(entry, picked, pos, wide, vec, start, normed, qkv, mixed, middle, normed_two):
    picks = picked[0]
    kept = jnp.sum(picks.astype(high_type), 1, keepdims=True)
    rows = place_rows(picks, entry[...]) + (1.0 - kept) * vec[1:2] + pos[...]
    start[...] = rows
    unit, _ = standard(rows)
    rows_in = (unit * vec[2:3] + vec[3:4]).astype(low_type)
    normed[...] = rows_in
    scale = 1.0 / math.sqrt(E // HD)
    qkv[:, :E] = ((nn(rows_in, wide[0, :, :E]) + vec[4:5]) * scale).astype(low_type)
    qkv[:, E : 2 * E] = nn(rows_in, wide[0, :, E : 2 * E]).astype(low_type)
    qkv[:, 2 * E :] = (nn(rows_in, wide[0, :, 2 * E : 3 * E]) + vec[5:6]).astype(low_type)
    heads = LANES * HD // E
    for group in range(E // LANES):
        lane = group * LANES
        mixed[:, lane : lane + LANES] = attend(
            qkv[:, lane : lane + LANES],
            qkv[:, E + lane : E + lane + LANES],
            qkv[:, 2 * E + lane : 2 * E + lane + LANES],
            heads,
            PATCHES + 1,
        ).astype(low_type)
    total = rows + (nn(mixed[...], wide[0, :, 3 * E :]) + vec[6:7])
    middle[...] = total
    unit, _ = standard(total)
    normed_two[...] = (unit * vec[7:8] + vec[8:9]).astype(low_type)


def send_tiles(acc, blob, sem, tiles, rows, per_block, base, stride):
    def go(index, carry):
        tile, part = index // 4, index % 4
        block, inner = tile // per_block, tile % per_block
        pltpu.make_async_copy(
            acc.at[tile, pl.ds(pl.multiple_of(part * rows, 16), rows)],
            blob.at[block, part, pl.ds(pl.multiple_of(base + inner * stride, 16), rows)],
            sem,
        ).start()
        return carry

    lax.fori_loop(0, tiles * 4, go, 0)


def wait_tiles(acc, sem):
    pltpu.make_async_copy(acc, acc, sem).wait()


def dec_ffn_kernel(images, last, count, middle, normed_two, mixed, pixels, picked, weights, head, vec, up_bias, head_bias,
                   grad_middle, grad_mixed, grad_head, vec_grad, up_grad, bias_grad, loss, blob,
                   active, slope, acc_up, acc_down, acc_out, sems):
    step = pl.program_id(0)
    source = normed_two[...]
    rows = source.shape[0]

    @pl.when(step == 0)
    def _():
        grad_head[...] = jnp.zeros_like(grad_head)
        vec_grad[...] = jnp.zeros_like(vec_grad)
        up_grad[...] = jnp.zeros_like(up_grad)
        bias_grad[...] = jnp.zeros_like(bias_grad)
        loss[...] = jnp.zeros_like(loss)
        acc_up[...] = jnp.zeros_like(acc_up)
        acc_down[...] = jnp.zeros_like(acc_down)
        acc_out[...] = jnp.zeros_like(acc_out)

    wide = 512
    total = middle[...] + vec[9:10]
    for place in range(0, H, wide):
        span = slice(place, place + wide)
        value, gain = gelu_pair(nn(source, weights[1, :, span]) + up_bias[:, span])
        slope[:, span] = gain
        value = value.astype(low_type)
        active[:, span] = value
        total = total + nt(value, weights[2, :, span])
    unit, rate = standard(total)
    final = (unit * vec[10:11] + vec[11:12]).astype(low_type)
    predict = nn(final, head[...]) + head_bias[...]
    target, _ = standard(pixels[...].astype(high_type))
    kept = jnp.concatenate([jnp.sum(picked[image].astype(high_type), 1, keepdims=True) for image in range(images)], 0)
    inner = lax.broadcasted_iota(jnp.int32, (rows, 1), 0) % DEC_ROWS
    masked = jnp.where(inner < PATCHES, 1.0 - kept, 0.0)
    error = predict - target
    loss[...] += jnp.sum(masked * error * error)
    grad_predict = (2.0 * masked * error / count).astype(low_type)
    grad_head[...] += tn(final, grad_predict)
    bias_grad[...] += col_sum(grad_predict)
    grad_final = nt(grad_predict, head[...])
    vec_grad[10:11] += col_sum(grad_final * unit)
    vec_grad[11:12] += col_sum(grad_final)
    grad_out = standard_back(unit, rate, grad_final * vec[10:11])
    grad_down = grad_out.astype(low_type)
    vec_grad[9:10] += col_sum(grad_down)
    grad_source = jnp.zeros_like(total)
    for place in range(0, H, wide):
        span = slice(place, place + wide)
        grad_up = (slope[:, span] * nn(grad_down, weights[2, :, span])).astype(low_type)
        up_grad[:, span] += col_sum(grad_up)
        grad_source = grad_source + nt(grad_up, weights[1, :, span])
        piece = tn(grad_down, active[:, span])
        other = tn(source, grad_up)
        for tile in range(wide // LANES):
            lane = slice(tile * LANES, (tile + 1) * LANES)
            acc_down[place // LANES + tile] += piece[:, lane]
            acc_up[place // LANES + tile] += other[:, lane]
    unit, rate = standard(middle[...])
    vec_grad[7:8] += col_sum(grad_source * unit)
    vec_grad[8:9] += col_sum(grad_source)
    grad_rows = standard_back(unit, rate, grad_source * vec[7:8]) + grad_out
    grad_middle[...] = grad_rows
    branch = grad_rows.astype(low_type)
    vec_grad[6:7] += col_sum(branch)
    piece = tn(mixed[...], branch)
    for tile in range(E // LANES):
        acc_out[tile] += piece[:, tile * LANES : (tile + 1) * LANES]
    grad_mixed[...] = nt(branch, weights[0, :, 3 * E :]).astype(low_type)

    @pl.when(step == last)
    def _():
        rows_block = E // 4
        send_tiles(acc_up, blob, sems.at[0], H // LANES, rows_block, 2, 2176, rows_block)
        send_tiles(acc_down, blob, sems.at[1], H // LANES, rows_block, 2, 2432, rows_block)
        send_tiles(acc_out, blob.at[pl.ds(6, 2)], sems.at[2], E // LANES, rows_block, 2, 1920, rows_block)
        wait_tiles(acc_up, sems.at[0])
        wait_tiles(acc_down, sems.at[1])
        wait_tiles(acc_out, sems.at[2])


def dec_back_kernel(last, blob_in, qkv, normed, start, grad_middle, grad_mixed, pick, picked, weights, vec,
                    grad_entry, vec_grad, blob, grads, acc, sem):
    step = pl.program_id(0)

    @pl.when(step == 0)
    def _():
        vec_grad[...] = jnp.zeros_like(vec_grad)
        acc[...] = jnp.zeros_like(acc)

    scale = 1.0 / math.sqrt(E // HD)
    heads = LANES * HD // E
    for group in range(E // LANES):
        lane = group * LANES
        span = slice(lane, lane + LANES)
        query, key, value = attend_back(
            qkv[:, lane : lane + LANES],
            qkv[:, E + lane : E + lane + LANES],
            qkv[:, 2 * E + lane : 2 * E + lane + LANES],
            grad_mixed[:, span],
            heads,
            PATCHES + 1,
        )
        grads[:, span] = (query * scale).astype(low_type)
        grads[:, E + lane : E + lane + LANES] = key.astype(low_type)
        grads[:, 2 * E + lane : 2 * E + lane + LANES] = value.astype(low_type)
    vec_grad[4:5] += col_sum(grads[:, :E])
    vec_grad[5:6] += col_sum(grads[:, 2 * E :])
    rows = normed[...]
    for part in range(3):
        piece = tn(rows, grads[:, part * E : (part + 1) * E])
        for tile in range(E // LANES):
            acc[part * (E // LANES) + tile] += piece[:, tile * LANES : (tile + 1) * LANES]
    grad_normed = nt(grads[...], weights[0, :, : 3 * E])
    unit, rate = standard(start[...])
    vec_grad[2:3] += col_sum(grad_normed * unit)
    vec_grad[3:4] += col_sum(grad_normed)
    grad_rows = standard_back(unit, rate, grad_normed * vec[2:3]) + grad_middle[...]
    kept = jnp.sum(picked[0].astype(high_type), 1, keepdims=True)
    vec_grad[1:2] += col_sum((1.0 - kept) * grad_rows)
    grad_entry[...] = nn(pick[0], grad_rows.astype(low_type)).astype(low_type)

    @pl.when(step == last)
    def _():
        rows_block = E // 4
        send_tiles(acc, blob, sem, 3 * E // LANES, rows_block, 2, 1920, rows_block)
        wait_tiles(acc, sem)


def enc_ffn_back_kernel(last, blob_in, grad_entry, latent, output, middle, normed_two, slope, active, ffn, proj, vec,
                        grad_middle, vec_grad, up_grad, entry_grad, blob,
                        grad_out, grad_down, grad_source, folded, acc_up, acc_down, fold_sem, sems):
    step = pl.program_id(0)
    fold_copy = pltpu.make_async_copy(folded, blob.at[:, :, pl.ds(2688, 96)], fold_sem)
    part_rows = D // 4

    @pl.when(step == 0)
    def _():
        vec_grad[...] = jnp.zeros_like(vec_grad)
        entries = grad_entry[...]
        entry_grad[...] = col_sum(entries)
        grad_proj = tn(latent[...], entries)
        lane = lax.broadcasted_iota(jnp.int32, (96, LANES), 1)
        for part in range(4):
            for pair in range(4):
                first = grad_proj[part * 192 : part * 192 + 96, pair * LANES : (pair + 1) * LANES]
                second = grad_proj[part * 192 + 96 : part * 192 + 192, pair * LANES : (pair + 1) * LANES]
                folded[2 * pair, part] = jnp.where(lane < 64, first, pltpu.roll(second, 64, 1))
                folded[2 * pair + 1, part] = jnp.where(lane < 64, pltpu.roll(first, 64, 1), second)
        fold_copy.start()
        grad_latent = nt(entries, proj[...])
        unit, rate = standard(output[...])
        vec_grad[10:11] = col_sum(grad_latent * unit)
        vec_grad[11:12] = col_sum(grad_latent)
        rows = standard_back(unit, rate, grad_latent * vec[10:11])
        grad_out[...] = rows
        grad_down[...] = rows.astype(low_type)
        vec_grad[9:10] = col_sum(rows.astype(low_type))
        grad_source[...] = jnp.zeros_like(grad_source)

    slot = step % 2

    @pl.when(step >= 2)
    def _():
        wait_tiles(acc_up.at[slot], sems.at[0, slot])
        wait_tiles(acc_down.at[slot], sems.at[1, slot])

    grads = grad_down[...]
    grad_up = (slope[...] * nn(grads, ffn[1])).astype(low_type)
    up_grad[...] = col_sum(grad_up)
    grad_source[...] += nt(grad_up, ffn[0])
    piece = tn(grads, active[...])
    other = tn(normed_two[...], grad_up)
    count = grad_up.shape[1] // LANES
    for tile in range(count):
        lane = slice(tile * LANES, (tile + 1) * LANES)
        acc_down[slot, tile] = piece[:, lane]
        acc_up[slot, tile] = other[:, lane]

    def go(index, carry):
        tile, part = index // 4, index % 4
        place = step * count + tile
        block, inner = place // 3, place % 3
        rows = pl.ds(pl.multiple_of(part * part_rows, 16), part_rows)
        for number, (acc, base) in enumerate(((acc_up, 768), (acc_down, 1344))):
            pltpu.make_async_copy(
                acc.at[slot, tile, rows],
                blob.at[block, part, pl.ds(pl.multiple_of(base + inner * part_rows, 16), part_rows)],
                sems.at[number, slot],
            ).start()
        return carry

    lax.fori_loop(0, count * 4, go, 0)

    @pl.when(step == last)
    def _():
        unit, rate = standard(middle[...])
        vec_grad[7:8] = col_sum(grad_source[...] * unit)
        vec_grad[8:9] = col_sum(grad_source[...])
        grad_rows = standard_back(unit, rate, grad_source[...] * vec[7:8]) + grad_out[...]
        grad_middle[...] = grad_rows
        vec_grad[6:7] = col_sum(grad_rows.astype(low_type))
        fold_copy.wait()
        for item in (0, 1):
            wait_tiles(acc_up.at[item], sems.at[0, item])
            wait_tiles(acc_down.at[item], sems.at[1, item])


def enc_back_kernel(batch, blob_in, qkv, kept, normed, start, mixed, grad_middle, wide, vec,
                    vec_grad, blob, grads, grad_wide, tiles, sem):
    rows = ENC_ROWS
    vec_grad[...] = jnp.zeros_like(vec_grad)
    branch = grad_middle[...].astype(low_type)
    grad_mixed = nt(branch, wide[:, 4 * D :]).astype(low_type)
    grad_wide[:, 4 * D :] = tn(mixed[...], branch)
    scale = 1.0 / math.sqrt(D // HE)
    heads = LANES * HE // D
    for group in range(D // LANES):
        lane = group * LANES
        query, key, value = attend_back_many(
            batch,
            qkv[:, lane : lane + LANES],
            qkv[:, D + lane : D + lane + LANES],
            qkv[:, 2 * D + lane : 2 * D + lane + LANES],
            grad_mixed[:, lane : lane + LANES],
            heads,
            KEEP + 1,
        )
        grads[:, lane : lane + LANES] = (query * scale).astype(low_type)
        grads[:, D + lane : D + lane + LANES] = key.astype(low_type)
        grads[:, 2 * D + lane : 2 * D + lane + LANES] = value.astype(low_type)
    vec_grad[4:5] = col_sum(grads[:, :D])
    vec_grad[5:6] = col_sum(grads[:, 2 * D :])
    rows_in = normed[...]
    for part in range(3):
        grad_wide[:, (part + 1) * D : (part + 2) * D] = tn(rows_in, grads[:, part * D : (part + 1) * D])
    width = 5 * D // 8
    tall = D // 4

    def assemble(block):
        for part in range(4):
            span = slice(part * tall, (part + 1) * tall)
            piece = grad_wide[span, block * width : (block + 1) * width]
            for tile in range(4):
                size = min(LANES, width - tile * LANES)
                value = piece[:, tile * LANES : tile * LANES + size]
                if size < LANES:
                    value = jnp.concatenate([value, jnp.zeros((tall, LANES - size), high_type)], 1)
                tiles[block, part, tile * tall : (tile + 1) * tall] = value
        pltpu.make_async_copy(tiles.at[block], blob.at[block, :, pl.ds(0, 4 * tall)], sem).start()

    for block in range(2, 8):
        assemble(block)
    grad_normed = nt(grads[...], wide[:, D : 4 * D])
    unit, rate = standard(start[...])
    vec_grad[2:3] = col_sum(grad_normed * unit)
    vec_grad[3:4] = col_sum(grad_normed)
    grad_rows = standard_back(unit, rate, grad_normed * vec[2:3]) + grad_middle[...]
    inner = lax.broadcasted_iota(jnp.int32, (grad_rows.shape[0], 1), 0) % rows
    vec_grad[1:2] = col_sum(jnp.where(inner == CLASS_ENC, grad_rows, 0.0))
    embed = jnp.where(inner < KEEP, grad_rows, 0.0).astype(low_type)
    vec_grad[0:1] = col_sum(embed)
    grad_wide[:, :D] = tn(kept[...], embed)
    assemble(0)
    assemble(1)
    wait_tiles(tiles, sem)


def adam_parts(weight, grad, first, second, decay):
    first_new = 0.5 * first + 0.5 * grad
    second_new = 0.5 * second + 0.5 * grad * grad
    bias = 1.0 - 0.5**STEP
    direction = first_new / bias / (jnp.sqrt(second_new / bias) + 1e-08)
    return weight - 0.02 * (direction + decay * weight), first_new, second_new


def adam_kernel(*refs):
    summed, head, small = refs[:3]
    ins, outs = refs[3:24], refs[24:]

    def update(index, place, grad, decay=0.05):
        for target, value in zip(
            range(3), adam_parts(ins[index][place], grad, ins[7 + index][place], ins[14 + index][place], decay)
        ):
            outs[7 * target + index][place] = value

    base = 0
    for index, lead, tall, width in ((0, None, 192, 480), (1, 0, 192, 384), (1, 1, 192, 384),
                                     (3, None, 128, 256), (4, 0, 128, 256), (4, 1, 128, 256)):
        for lane in range(0, width, LANES):
            size = min(LANES, width - lane)
            place = (slice(None), slice(lane, lane + size))
            update(index, place if lead is None else (lead,) + place, summed[base : base + tall, :size])
            base += tall
    folded = summed[base : base + 96]
    update(2, (slice(0, 96),), folded[:, :64])
    update(2, (slice(96, 192),), folded[:, 64:])
    update(5, (slice(None),), head[...])
    update(6, (slice(None),), small[...], 0.0)


def table_of(width, rows):
    quarter = width // 4
    omega = (np.float32(1.0) / np.float32(10000.0) ** (np.arange(quarter, dtype=np.float32) / np.float32(quarter))).astype(np.float32)
    coord = np.arange(SIDE * SIDE)

    def half(place):
        angle = place.astype(np.float32)[:, None] * omega[None, :]
        return np.concatenate([np.sin(angle), np.cos(angle)], 1)

    table = np.concatenate([half(coord // SIDE), half(coord % SIDE)], 1).astype(np.float32)
    return np.concatenate([table, np.zeros((rows - table.shape[0], width), np.float32)], 0)


def whole():
    return pl.BlockSpec(memory_space=pltpu.VMEM)


def hbm():
    return pl.BlockSpec(memory_space=pltpu.HBM)


def params(**more):
    return pltpu.CompilerParams(vmem_limit_bytes=60 << 20, **more)


def local_grads(enc_blocks, enc_ffn, proj, dec3, head_low, smalls_parts, patches, shuffle, count):
    enc_vec, enc_up, dec_vec, dec_up, head_bias = smalls_parts
    enc_up, dec_up, head_bias = enc_up[None], dec_up[None], head_bias[None]
    batch = patches.shape[0]
    shape = jax.ShapeDtypeStruct
    keep = jnp.concatenate(
        [
            shuffle[:, :KEEP],
            jnp.full((batch, 1), CLASS_DEC, jnp.int32),
            jnp.full((batch, ENC_ROWS - KEEP - 1), -1, jnp.int32),
        ],
        1,
    )
    places = jnp.arange(DEC_ROWS, dtype=jnp.int32)
    pick = (keep[:, :, None] == places[None, None, :]).astype(low_type)
    picked = (keep[:, None, :] == places[None, :, None]).astype(low_type)
    padded = jnp.pad(patches, ((0, 0), (0, DEC_ROWS - PATCHES), (0, 0)))
    enc_pos = jnp.asarray(table_of(D, DEC_ROWS))
    dec_pos = jnp.asarray(table_of(E, DEC_ROWS))
    rows, dec_rows = batch * ENC_ROWS, batch * DEC_ROWS

    wide = pl.pallas_call(
        wide_kernel,
        out_shape=shape((D, 5 * D), low_type),
        in_specs=[whole()],
        out_specs=whole(),
        compiler_params=params(),
        name="wide",
    )(enc_blocks)
    kept, start, normed, qkv, mixed, middle, normed_two = pl.pallas_call(
        functools.partial(enc_attend_kernel, batch),
        out_shape=(
            shape((rows, D), low_type),
            shape((rows, D), high_type),
            shape((rows, D), low_type),
            shape((rows, 3 * D), low_type),
            shape((rows, D), low_type),
            shape((rows, D), high_type),
            shape((rows, D), low_type),
        ),
        in_specs=[whole()] * 5,
        out_specs=[whole()] * 7,
        compiler_params=params(),
        name="enc_attend",
    )(pick, padded, wide, enc_vec, enc_pos)
    def by_image(*block):
        return pl.BlockSpec(block, lambda i: (i,) + (0,) * (len(block) - 1))

    def fixed(*block):
        return pl.BlockSpec(block, lambda i: (0,) * len(block))

    chunk = 512
    rows_whole = lambda width: fixed(rows, width)
    slope, active, enc_out, latent, entry = pl.pallas_call(
        functools.partial(enc_ffn_kernel, F // chunk - 1),
        grid=(F // chunk,),
        out_shape=(
            shape((rows, F), high_type),
            shape((rows, F), low_type),
            shape((rows, D), high_type),
            shape((rows, D), low_type),
            shape((rows, E), high_type),
        ),
        in_specs=[
            rows_whole(D),
            rows_whole(D),
            pl.BlockSpec((2, D, chunk), lambda i: (0, 0, i)),
            fixed(12, D),
            pl.BlockSpec((1, chunk), lambda i: (0, i)),
            fixed(D, E),
            fixed(12, E),
        ],
        out_specs=[
            pl.BlockSpec((rows, chunk), lambda i: (0, i)),
            pl.BlockSpec((rows, chunk), lambda i: (0, i)),
            rows_whole(D),
            rows_whole(D),
            rows_whole(E),
        ],
        compiler_params=params(),
        name="enc_ffn",
    )(middle, normed_two, enc_ffn, enc_vec, enc_up, proj, dec_vec)

    dec_start, dec_normed, dec_qkv, dec_mixed, dec_middle, dec_normed_two = pl.pallas_call(
        dec_attend_kernel,
        grid=(batch,),
        out_shape=(
            shape((dec_rows, E), high_type),
            shape((dec_rows, E), low_type),
            shape((dec_rows, 3 * E), low_type),
            shape((dec_rows, E), low_type),
            shape((dec_rows, E), high_type),
            shape((dec_rows, E), low_type),
        ),
        in_specs=[
            by_image(ENC_ROWS, E),
            by_image(1, DEC_ROWS, ENC_ROWS),
            fixed(DEC_ROWS, E),
            fixed(1, E, 4 * E),
            fixed(12, E),
        ],
        out_specs=[
            by_image(DEC_ROWS, E),
            by_image(DEC_ROWS, E),
            by_image(DEC_ROWS, 3 * E),
            by_image(DEC_ROWS, E),
            by_image(DEC_ROWS, E),
            by_image(DEC_ROWS, E),
        ],
        compiler_params=params(),
        name="dec_attend",
    )(entry, picked, dec_pos, dec3, dec_vec)

    images = 2 if batch % 2 == 0 else 1
    block = images * DEC_ROWS
    blob_shape = shape((8, 4, 2784, LANES), high_type)
    vm = pltpu.VMEM
    dma = pltpu.SemaphoreType.DMA
    grad_middle, grad_mixed, grad_head, dec_grad_one, dec_up_grad, head_bias_grad, loss, blob = pl.pallas_call(
        functools.partial(dec_ffn_kernel, images, batch // images - 1, count),
        grid=(batch // images,),
        out_shape=(
            shape((dec_rows, E), high_type),
            shape((dec_rows, E), low_type),
            shape((E, P_SIZE), high_type),
            shape((12, E), high_type),
            shape((1, H), high_type),
            shape((1, P_SIZE), high_type),
            shape((8, LANES), high_type),
            blob_shape,
        ),
        in_specs=[
            by_image(block, E),
            by_image(block, E),
            by_image(block, E),
            by_image(block, P_SIZE),
            by_image(images, DEC_ROWS, ENC_ROWS),
            fixed(3, E, H),
            fixed(E, P_SIZE),
            fixed(12, E),
            fixed(1, H),
            fixed(1, P_SIZE),
        ],
        out_specs=[
            by_image(block, E),
            by_image(block, E),
            fixed(E, P_SIZE),
            fixed(12, E),
            fixed(1, H),
            fixed(1, P_SIZE),
            fixed(8, LANES),
            hbm(),
        ],
        scratch_shapes=[
            vm((block, H), low_type),
            vm((block, H), high_type),
            vm((H // LANES, E, LANES), high_type),
            vm((H // LANES, E, LANES), high_type),
            vm((E // LANES, E, LANES), high_type),
            dma((3,)),
        ],
        compiler_params=params(),
        name="dec_ffn",
    )(dec_middle, dec_normed_two, dec_mixed, padded.reshape(dec_rows, P_SIZE), picked, dec3, head_low, dec_vec, dec_up, head_bias)

    grad_entry, dec_grad_two, blob = pl.pallas_call(
        functools.partial(dec_back_kernel, batch - 1),
        grid=(batch,),
        out_shape=(shape((rows, E), low_type), shape((12, E), high_type), blob_shape),
        in_specs=[
            hbm(),
            by_image(DEC_ROWS, 3 * E),
            by_image(DEC_ROWS, E),
            by_image(DEC_ROWS, E),
            by_image(DEC_ROWS, E),
            by_image(DEC_ROWS, E),
            by_image(1, ENC_ROWS, DEC_ROWS),
            by_image(1, DEC_ROWS, ENC_ROWS),
            fixed(1, E, 4 * E),
            fixed(12, E),
        ],
        out_specs=[by_image(ENC_ROWS, E), fixed(12, E), hbm()],
        scratch_shapes=[vm((DEC_ROWS, 3 * E), low_type), vm((3 * E // LANES, E, LANES), high_type), dma],
        input_output_aliases={0: 2},
        compiler_params=params(),
        name="dec_back",
    )(blob, dec_qkv, dec_normed, dec_start, grad_middle, grad_mixed, pick, picked, dec3, dec_vec)

    enc_grad_middle, enc_grad_one, enc_up_grad, entry_grad, blob = pl.pallas_call(
        functools.partial(enc_ffn_back_kernel, F // chunk - 1),
        grid=(F // chunk,),
        out_shape=(
            shape((rows, D), high_type),
            shape((12, D), high_type),
            shape((1, F), high_type),
            shape((1, E), high_type),
            blob_shape,
        ),
        in_specs=[
            hbm(),
            rows_whole(E),
            rows_whole(D),
            rows_whole(D),
            rows_whole(D),
            rows_whole(D),
            pl.BlockSpec((rows, chunk), lambda i: (0, i)),
            pl.BlockSpec((rows, chunk), lambda i: (0, i)),
            pl.BlockSpec((2, D, chunk), lambda i: (0, 0, i)),
            fixed(D, E),
            fixed(12, D),
        ],
        out_specs=[
            rows_whole(D),
            fixed(12, D),
            pl.BlockSpec((1, chunk), lambda i: (0, i)),
            fixed(1, E),
            hbm(),
        ],
        scratch_shapes=[
            vm((rows, D), high_type),
            vm((rows, D), low_type),
            vm((rows, D), high_type),
            vm((8, 4, 96, LANES), high_type),
            vm((2, chunk // LANES, D, LANES), high_type),
            vm((2, chunk // LANES, D, LANES), high_type),
            dma,
            dma((2, 2)),
        ],
        input_output_aliases={0: 4},
        compiler_params=params(),
        name="enc_ffn_back",
    )(blob, grad_entry, latent, enc_out, middle, normed_two, slope, active, enc_ffn, proj, enc_vec)
    enc_grad_two, blob = pl.pallas_call(
        functools.partial(enc_back_kernel, batch),
        out_shape=(shape((12, D), high_type), blob_shape),
        in_specs=[hbm()] + [whole()] * 8,
        out_specs=[whole(), hbm()],
        scratch_shapes=[
            vm((rows, 3 * D), low_type),
            vm((D, 5 * D), high_type),
            vm((8, 4, D, LANES), high_type),
            dma,
        ],
        input_output_aliases={0: 1},
        compiler_params=params(),
        name="enc_back",
    )(blob, qkv, kept, normed, start, mixed, enc_grad_middle, wide, enc_vec)
    dec_grad = (dec_grad_one + dec_grad_two).at[0].set(entry_grad[0])
    smalls = jnp.concatenate(
        [
            (enc_grad_one + enc_grad_two).reshape(-1),
            enc_up_grad[0],
            dec_grad.reshape(-1),
            dec_up_grad[0],
            head_bias_grad[0],
        ]
    )
    return blob, grad_head, smalls, loss[0, 0]


def untile(block, rows, width):
    tiles = -(-width // LANES)
    return block.reshape(tiles, rows, LANES).transpose(1, 0, 2).reshape(rows, tiles * LANES)[:, :width]


def unfold_proj(block):
    width = block.shape[1] // 2
    return jnp.concatenate([block[:, :width], block[:, width:]], 0)


def unpack_shards(blob):
    cuts = [0, 768, 576, 576, 256, 256, 256, 96]
    places = [sum(cuts[: index + 1]) for index in range(len(cuts))]
    piece = [blob[places[index] : places[index + 1]] for index in range(7)]
    return (
        untile(piece[0], 192, 480),
        jnp.stack([untile(piece[1], 192, 384), untile(piece[2], 192, 384)]),
        unfold_proj(piece[6]),
        untile(piece[3], 128, 256),
        jnp.stack([untile(piece[4], 128, 256), untile(piece[5], 128, 256)]),
    )


def whole_arrays(blob):
    col_size, row_size = blob.shape[:2]
    parts = jax.vmap(jax.vmap(unpack_shards))(blob)

    def joined(array):
        if array.ndim == 4:
            return array.transpose(1, 2, 0, 3).reshape(row_size * array.shape[2], col_size * array.shape[3])
        return array.transpose(2, 1, 3, 0, 4).reshape(2, row_size * array.shape[3], col_size * array.shape[4])

    return tuple(joined(item) for item in parts)


def on_small_plane():
    return lax.axis_size("row") == 4 and lax.axis_size("col") == 8


def gather_weights(enc_w, enc_ffn, dec_proj, dec_w, dec_ffn):
    shards = [item.astype(low_type) for item in (enc_w, enc_ffn, dec_proj, jnp.concatenate([dec_w[None], dec_ffn], 0))]
    if on_small_plane():
        enc, ffn, proj, dec = gather_blocks(*shards, lax.axis_size("col") // 2)
        return enc, ffn, proj.transpose(1, 0, 2).reshape(D, E), dec
    full = []
    for item in shards:
        rowed = lax.all_gather(item, "row", axis=item.ndim - 2, tiled=True)
        full.append(lax.all_gather(rowed, "col", axis=item.ndim - 1, tiled=True))
    return full[0].reshape(D, 8, 5 * D // 8).transpose(1, 0, 2), full[1], full[2], full[3]


def apply_updates(blob, grad_head, smalls, loss, params_now, firsts, seconds):
    count = smalls.shape[0]
    summed_head = lax.psum(grad_head, ("row", "col"))
    if on_small_plane():
        small = jnp.concatenate([smalls, loss[None], jnp.zeros((32 * 8 * LANES - count - 1,), high_type)])
        summed, small = reduce_blocks(blob, small.reshape(32, 8, LANES), lax.axis_size("col") // 2, 6)
        small = small.reshape(-1, LANES)
        flat = lambda group: group[:6] + (group[6].reshape(-1, LANES),)
        ins = flat(params_now) + flat(firsts) + flat(seconds)
        outs = pl.pallas_call(
            adam_kernel,
            out_shape=tuple(jax.ShapeDtypeStruct(item.shape, high_type) for item in ins),
            in_specs=[whole()] * 24,
            out_specs=[whole()] * 21,
            compiler_params=params(),
            name="adam",
        )(summed, summed_head, small[: count // LANES], *ins)
        outs = [item.reshape(-1) if index % 7 == 6 else item for index, item in enumerate(outs)]
        return outs, small[count // LANES, count % LANES]
    shards = []
    for item in whole_arrays(blob):
        done = lax.psum_scatter(item, "col", scatter_dimension=item.ndim - 1, tiled=True)
        shards.append(lax.psum_scatter(done, "row", scatter_dimension=item.ndim - 2, tiled=True))
    smalls, loss = lax.psum((smalls, loss), ("row", "col"))
    grads = tuple(shards) + (summed_head, smalls)
    decays = (0.05,) * 6 + (0.0,)
    results = [adam_parts(*item) for item in zip(params_now, grads, firsts, seconds, decays)]
    return [item[kind] for kind in range(3) for item in results], loss


def body(
    patches,
    shuffle,
    enc_w,
    enc_ffn,
    dec_proj,
    dec_w,
    dec_ffn,
    head_w,
    smalls,
    first_enc_w,
    first_enc_ffn,
    first_dec_proj,
    first_dec_w,
    first_dec_ffn,
    first_head_w,
    first_smalls,
    second_enc_w,
    second_enc_ffn,
    second_dec_proj,
    second_dec_w,
    second_dec_ffn,
    second_head_w,
    second_smalls,
):
    enc_blocks, enc_ffn_w, proj, dec3 = gather_weights(enc_w, enc_ffn, dec_proj, dec_w, dec_ffn)
    count = patches.shape[0] * lax.axis_size("row") * lax.axis_size("col") * (PATCHES - KEEP) * P_SIZE
    blob, grad_head, grad_smalls, loss_local = local_grads(
        enc_blocks, enc_ffn_w, proj, dec3, head_w.astype(low_type), unpack(smalls), patches, shuffle, count
    )
    params_now = (enc_w, enc_ffn, dec_proj, dec_w, dec_ffn, head_w, smalls)
    firsts = (
        first_enc_w,
        first_enc_ffn,
        first_dec_proj,
        first_dec_w,
        first_dec_ffn,
        first_head_w,
        first_smalls,
    )
    seconds = (
        second_enc_w,
        second_enc_ffn,
        second_dec_proj,
        second_dec_w,
        second_dec_ffn,
        second_head_w,
        second_smalls,
    )
    outs, loss_sum = apply_updates(blob, grad_head, grad_smalls, loss_local, params_now, firsts, seconds)
    return tuple(outs) + (loss_sum / count,)


def solution(mesh):
    in_specs = (
        P(("row", "col"), None, None),
        P(("row", "col"), None),
        P("row", "col"),
        P(None, "row", "col"),
        P("row", "col"),
        P("row", "col"),
        P(None, "row", "col"),
        P(),
        P(),
        P("row", "col"),
        P(None, "row", "col"),
        P("row", "col"),
        P("row", "col"),
        P(None, "row", "col"),
        P(),
        P(),
        P("row", "col"),
        P(None, "row", "col"),
        P("row", "col"),
        P("row", "col"),
        P(None, "row", "col"),
        P(),
        P(),
    )
    out_specs = (
        P("row", "col"),
        P(None, "row", "col"),
        P("row", "col"),
        P("row", "col"),
        P(None, "row", "col"),
        P(),
        P(),
        P("row", "col"),
        P(None, "row", "col"),
        P("row", "col"),
        P("row", "col"),
        P(None, "row", "col"),
        P(),
        P(),
        P("row", "col"),
        P(None, "row", "col"),
        P("row", "col"),
        P("row", "col"),
        P(None, "row", "col"),
        P(),
        P(),
        P(),
    )
    return jax.shard_map(body, mesh=mesh, in_specs=in_specs, out_specs=out_specs, check_vma=False)
```

profile of v0, /device:TPU:0, one launch (start us, length us, event | category | flops | bytes accessed | tf_op | source)
XLA Modules:
  0.0 458.7 jit_solution(11455263276435664302)
XLA Ops:
  7.3 1.4 slice.44
  11.1 1.3 slice.46
  17.2 108.9 %gather_blocks.1 = (bf16[8,768,480]{2,1,0:T(8,128)(2,1)}, bf16[2,768,3072]{2,1,0:T(8,128)(2,1)}, bf16[8,768,64]{2,1,0:T(8,128)(2,1)}, bf16[3,512,2048]{2,1,0:T(8,128)(2,1)}) custom-call(bf16[192,480]{1,0:T(8,128)(2,1)} %convert_element_type.22.own_enc, bf16[2,192,384]{2,1,0:T(8,128)(2,1)} %convert_element_type.23.own_ffn, bf16[192,64]{1,0:T(8,128)(2,1)} %copy.68.own_proj, ...), custom_call_target="tpu_custom_call" | custom-call | tf_op jit(solution)/shard_map/gather_blocks/pallas_call | solution.py:259
  126.0 6.5 %wide.1 = bf16[768,3840]{1,0:T(8,128)(2,1)} custom-call(bf16[8,768,480]{2,1,0:T(8,128)(2,1)} %get-tuple-element.97.blocks), custom_call_target="tpu_custom_call" | custom-call | tf_op jit(solution)/shard_map/wide/pallas_call | solution.py:1165
  133.2 2.2 copy.69
  135.4 1.2 copy.70.proj
  139.0 1.4 pad.6.patches
  140.4 11.4 %enc_attend.1 = (bf16[384,768]{1,0:T(8,128)(2,1)}, f32[384,768]{1,0:T(8,128)}, bf16[384,768]{1,0:T(8,128)(2,1)}, bf16[384,2304]{1,0:T(8,128)(2,1)}, bf16[384,768...) custom-call(bf16[6,64,208]{2,1,0:T(8,128)(2,1)} %fusion.1.pick, bf16[6,208,768]{2,1,0:T(8,128)(2,1)} %pad.6.patches, ...), custom_call_target="tpu_custom_call" | custom-call | tf_op jit(solution)/shard_map/enc_attend/pallas_call | solution.py:1173
  151.8 14.9 %enc_ffn.1 = (f32[384,3072]{1,0:T(8,128)}, bf16[384,3072]{1,0:T(8,128)(2,1)}, f32[384,768]{1,0:T(8,128)}, bf16[384,768]{1,0:T(8,128)(2,1)}, f32[384,512]{1,0:T(8,128)}) custom-call(f32[384,768]{1,0:T(8,128)} %get-tuple-element.98.middle, bf16[384,768]{1,0:T(8,128)(2,1)} %get-tuple-element.99.normed_two, bf16[2,768,3072]{2,1,0:T(8,128)(2,1)} %get-tuple-element.100.ffn, ...), custom_call_target="tpu_custom_call" | custom-call | tf_op jit(solution)/shard_map/enc_ffn/pallas_call | solution.py:1197
  166.8 21.9 %dec_attend.1 = (f32[1248,512]{1,0:T(8,128)}, bf16[1248,512]{1,0:T(8,128)(2,1)}, bf16[1248,1536]{1,0:T(8,128)(2,1)}, bf16[1248,512]{1,0:T(8,128)(2,1)}, f32[1248,512]{1,0:T(8,128)}, /*index=5*/bf16[1248,512]{1,0:T(8,128)(2,1)}) custom-call(f32[384,512]{1,0:T(8,128)} %get-tuple-element.102.entry, bf16[6,208,64]{2,1,0:T(8,128)(2,1)} %fusion.picked, ...), custom_call_target="tpu_custom_call" | custom-call | tf_op jit(solution)/shard_map/dec_attend/pallas_call | solution.py:1227
  188.7 46.8 %dec_ffn.1 = (f32[1248,512]{1,0:T(8,128)}, bf16[1248,512]{1,0:T(8,128)(2,1)}, f32[512,768]{1,0:T(8,128)}, f32[12,512]{1,0:T(8,128)}, f32[1,2048]{1,0:T(1,128)}, ...) custom-call(f32[1248,512]{1,0:T(8,128)} %get-tuple-element.104.middle, ...), custom_call_target="tpu_custom_call" | custom-call | tf_op jit(solution)/shard_map/dec_ffn/pallas_call | solution.py:1262
  236.3 29.9 %dec_back.1 = (bf16[384,512]{1,0:T(8,128)(2,1)}, f32[12,512]{1,0:T(8,128)}, f32[8,4,2784,128]{3,2,1,0:T(8,128)}) custom-call(f32[8,4,2784,128]{3,2,1,0:T(8,128)} %get-tuple-element.107.blob_in, bf16[1248,1536]{1,0:T(8,128)(2,1)} %get-tuple-element.108.qkv, bf16[1248,512]{1,0:T(8,128)(2,1)} %get-tuple-element.109.normed, ...), custom_call_target="tpu_custom_call", output_to_operand_aliasing={{2}: (0, {})} | custom-call | tf_op jit(solution)/shard_map/dec_back/pallas_call | solution.py:1309
  267.1 21.1 %enc_ffn_back.1 = (f32[384,768]{1,0:T(8,128)}, f32[12,768]{1,0:T(8,128)}, f32[1,3072]{1,0:T(1,128)}, f32[1,512]{1,0:T(1,128)}, f32[8,4,2784,128]{3,2,1,0:T(8,128)}) custom-call(f32[8,4,2784,128]{3,2,1,0:T(8,128)} %get-tuple-element.113.blob_in, bf16[384,512]{1,0:T(8,128)(2,1)} %get-tuple-element.114.grad_entry, ...), custom_call_target="tpu_custom_call", output_to_operand_aliasing={{4}: (0, {})} | custom-call | tf_op jit(solution)/shard_map/enc_ffn_back/pallas_call | solution.py:1332
  288.2 1.1 scatter.4
  289.4 16.2 %enc_back.1 = (f32[12,768]{1,0:T(8,128)}, f32[8,4,2784,128]{3,2,1,0:T(8,128)}) custom-call(f32[8,4,2784,128]{3,2,1,0:T(8,128)} %get-tuple-element.119.blob_in, bf16[384,2304]{1,0:T(8,128)(2,1)} %get-tuple-element.120.qkv, bf16[384,768]{1,0:T(8,128)(2,1)} %get-tuple-element.121.kept, ...), custom_call_target="tpu_custom_call", output_to_operand_aliasing={{1}: (0, {})} | custom-call | tf_op jit(solution)/shard_map/enc_back/pallas_call | solution.py:1376
  306.4 1.2 slice.48
  307.7 1.4 concatenate.14
  309.1 121.0 %reduce_blocks.1 = (f32[2784,128]{1,0:T(8,128)}, f32[32,8,128]{2,1,0:T(8,128)}) custom-call(f32[8,4,2784,128]{3,2,1,0:T(8,128)} %get-tuple-element.126.blob, f32[32,8,128]{2,1,0:T(8,128)} %bitcast.23), custom_call_target="tpu_custom_call" | custom-call | tf_op jit(solution)/shard_map/reduce_blocks/pallas_call | solution.py:548
  430.1 1.5 slice.51.refs_2_
  431.6 1.2 slice.52
  435.0 10.7 %adam.1 = (f32[192,480]{1,0:T(8,128)}, f32[2,192,384]{2,1,0:T(8,128)}, f32[192,64]{1,0:T(8,128)}, f32[128,256]{1,0:T(8,128)}, f32[2,128,256]{2,1,0:T(8,128)}, /*...) custom-call(f32[2784,128]{1,0:T(8,128)} %get-tuple-element.136.refs_, ...), custom_call_target="tpu_custom_call" | custom-call | tf_op jit(solution)/shard_map/adam/pallas_call | solution.py:1464
  445.7 1.6 copy.75
  447.3 1.6 copy.76
  448.9 1.6 copy.77
  (60 shorter events, 14.2 us)
Async XLA Ops:
  7.2 7.1 %copy-start.1 = (f32[2,192,384]{2,1,0:T(8,128)S(1)}, f32[2,192,384]{2,1,0:T(8,128)}, u32[]{:S(2)}) copy-start(f32[2,192,384]{2,1,0:T(8,128)} %refs_4_.1) | copy-start | bytes 1769476
  7.2 7.8 %copy-start.3 = (f32[192,480]{1,0:T(8,128)S(1)}, f32[192,480]{1,0:T(8,128)}, u32[]{:S(2)}) copy-start(f32[192,480]{1,0:T(8,128)} %refs_3_.1) | copy-start | bytes 1105924
  7.2 8.5 %copy-start.4 = (f32[192,64]{0,1:T(8,128)S(1)}, f32[192,64]{0,1:T(8,128)}, u32[]{:S(2)}) copy-start(f32[192,64]{0,1:T(8,128)} %param.31) | copy-start | bytes 147460
  7.2 427.8 %all-reduce.3.cloned.1.call-start = ((), (), s32[]{:S(2)}) async-start(), calls=%async_computation | async-start | bytes 3145728 | tf_op jit(solution)/shard_map/psum | solution.py:1457
  126.0 6.6 %slice-start = ((f32[21248]{0:T(1024)}), f32[9216]{0:T(1024)S(1)}, s32[]{:S(2)}) async-start(f32[21248]{0:T(1024)} %param.35), calls=%async_computation.1 | async-start | bytes 73728 | tf_op jit(solution)/shard_map/slice | solution.py:36
  133.2 3.4 slice-start.1
  133.2 4.0 copy-start
  136.6 1.7 slice-start.2
  137.2 1.8 copy-start.2
  236.3 29.9 %copy-start.8 = (f32[12,512]{1,0:T(8,128)S(1)}, f32[12,512]{1,0:T(8,128)}, u32[]{:S(2)}) copy-start(f32[12,512]{1,0:T(8,128)} %get-tuple-element.130) | copy-start | bytes 73732
  289.3 16.3 %copy-start.7 = (f32[12,768]{1,0:T(8,128)S(1)}, f32[12,768]{1,0:T(8,128)}, u32[]{:S(2)}) copy-start(f32[12,768]{1,0:T(8,128)} %get-tuple-element.127) | copy-start | bytes 110596
  289.4 18.3 %copy-start.11 = (f32[1,768]{1,0:T(1,128)S(1)}, f32[1,768]{1,0:T(1,128)}, u32[]{:S(2)}) copy-start(f32[1,768]{1,0:T(1,128)} %get-tuple-element.134) | copy-start | bytes 9220
  289.4 18.3 %copy-start.9 = (f32[1,3072]{1,0:T(1,128)S(1)}, f32[1,3072]{1,0:T(1,128)}, u32[]{:S(2)}) copy-start(f32[1,3072]{1,0:T(1,128)} %get-tuple-element.129) | copy-start | bytes 36868
  289.4 18.3 %copy-start.10 = (f32[1,2048]{1,0:T(1,128)S(1)}, f32[1,2048]{1,0:T(1,128)}, u32[]{:S(2)}) copy-start(f32[1,2048]{1,0:T(1,128)} %get-tuple-element.133) | copy-start | bytes 24580
  309.1 123.7 %copy-start.5 = (f32[192,64]{0,1:T(8,128)S(1)}, f32[192,64]{0,1:T(8,128)}, u32[]{:S(2)}) copy-start(f32[192,64]{0,1:T(8,128)} %param.38) | copy-start | bytes 147460
  309.1 124.5 %copy-start.6 = (f32[192,64]{0,1:T(8,128)S(1)}, f32[192,64]{0,1:T(8,128)}, u32[]{:S(2)}) copy-start(f32[192,64]{0,1:T(8,128)} %param.45) | copy-start | bytes 147460
Sparse Core Ops, SparseCore 0:
  235.7 131.7 all-reduce.2
where the time goes:
time: 464 us; the launch traced here: 459 us
  Pallas kernels  410 us (88%)
  local copies, waits for them, and re-layouts  24.6 us (5%)
  between operations  16.3 us (4%)
  other arithmetic  8.26 us (2%)
    pallas_call x1, Pallas kernels, reduce_blocks(): pl.pallas_call(functools.partial(reduce_kernel, depth, devices, cols, par...  121 us
    pallas_call x1, Pallas kernels, gather_blocks(): pl.pallas_call(functools.partial(gather_kernel, depth), out_shape=(shape(...  109 us
    pallas_call x1, Pallas kernels, local_grads(): pl.pallas_call(functools.partial(dec_ffn_kernel, images, batch // images...  46.8 us
    pallas_call x1, Pallas kernels, local_grads(): pl.pallas_call(functools.partial(dec_back_kernel, batch - 1), grid=(batch...  29.9 us
    pallas_call x1, Pallas kernels, local_grads(): pl.pallas_call(dec_attend_kernel, grid=(batch,), out_shape=(shape((dec_ro...  21.9 us
    pallas_call x1, Pallas kernels, local_grads(): pl.pallas_call(functools.partial(enc_ffn_back_kernel, F // chunk - 1), gr...  21.1 us
    pallas_call x1, Pallas kernels, local_grads(): pl.pallas_call(functools.partial(enc_back_kernel, batch), out_shape=(shap...  16.2 us
    pallas_call x1, Pallas kernels, local_grads(): pl.pallas_call(functools.partial(enc_ffn_kernel, F // chunk - 1), grid=(F...  14.9 us
  transfers between devices with their start and end apart: 1, of which 0 were waited for; matrix products, arithmetic and copies ran while one was open for 2% of the time, Pallas kernels for 41%

commit v1 on v0

--- a/solution.py
+++ b/solution.py
@@ -42,6 +42,7 @@
 
 
 MESH = pl.DeviceIdType.MESH
+LAGS = (2, 4, 6)
 
 
 class Group:
@@ -65,34 +66,9 @@
             item.wait()
 
 
-def gather_kernel(depth, own_enc, own_ffn, own_proj, own_dec, enc, ffn, proj, dec,
-                  zs, zr, xs, xr, ys, yr, dxs, dxr, dys, dyr, cs, cr, local):
-    row = lax.axis_index("row")
-    col = lax.axis_index("col")
-    y, x, z, k = row // 2, row % 2, col // 2, col % 2
-    row_x = y * 2 + (1 - x)
-    row_y = (1 - y) * 2 + x
-    row_d = (1 - y) * 2 + (1 - x)
-    near_x, near_y = (row_x, col), (row_y, col)
-    twin = (row, z * 2 + (1 - k))
-    lower, upper = (row, col - 2), (row, col + 2)
-    has_lower, has_upper = z > 0, z < depth - 1
-    own = (own_enc, own_ffn, own_proj, own_dec)
-
-    barrier = pltpu.get_barrier_semaphore()
-    for other in (near_x, near_y, twin):
-        pl.semaphore_signal(barrier, inc=1, device_id=other, device_id_type=MESH)
-
-    @pl.when(has_lower)
-    def _():
-        pl.semaphore_signal(barrier, inc=1, device_id=lower, device_id_type=MESH)
-
-    @pl.when(has_upper)
-    def _():
-        pl.semaphore_signal(barrier, inc=1, device_id=upper, device_id_type=MESH)
-
-    pl.semaphore_wait(barrier, 3 + jnp.where(has_lower, 1, 0) + jnp.where(has_upper, 1, 0))
-
+def gather_steps(depth, place_ids, own, cut, sems):
+    row, row_x, row_y, row_d, z, k, near_x, near_y, twin, lower, upper, has_lower, has_upper = place_ids
+    zs, zr, xs, xr, ys, yr, dxs, dxr, dys, dyr, cs, cr = sems
     levels = [(0, 0)] + [(d, way) for d in range(1, depth) for way in (0, 1)]
     level_of = {item: number for number, item in enumerate(levels)}
 
@@ -103,21 +79,6 @@
     def valid(level):
         d, way = level
         return z - d >= 0 if way == 0 else z + d < depth
-
-    def cut(index, row_now, half=None):
-        def rows(size, unit):
-            part = size if half is None else size // 2
-            first = 0 if half is None else half * part
-            return pl.ds(pl.multiple_of(row_now * size + first, 16), part)
-
-        tall, short = own_enc.shape[0], own_dec.shape[1]
-        wide, thin = own_ffn.shape[2], own_dec.shape[2]
-        return (
-            enc.at[index, rows(tall, 16)],
-            ffn.at[:, rows(tall, 16), pl.ds(pl.multiple_of(index * wide, LANES), wide)],
-            proj.at[index, rows(tall, 16)],
-            dec.at[:, rows(short, 16), pl.ds(pl.multiple_of(index * thin, LANES), thin)],
-        )
 
     def slot(level, row_now, half=None):
         return cut(place(level) * 2 + k, row_now, half)
@@ -136,7 +97,7 @@
                     device_id=target,
                     device_id_type=MESH,
                 )
-                for item in range(4)
+                for item in range(len(own))
             ]
         )
 
@@ -229,11 +190,7 @@
 
         guarded(level, action)
 
-    keep = Group(
-        [pltpu.make_async_copy(src, dst, local.at[item]) for item, (src, dst) in enumerate(zip(own, cut(col, row)))]
-    )
-    keep.start()
-    for step in range(depth + 2):
+    def step_action(step):
         for level in levels:
             if level[0] == step:
                 spread(level)
@@ -243,35 +200,179 @@
         for level in levels:
             if level[0] == step - 2:
                 close(level)
-    keep.wait()
-    for level in levels:
-        drain(level)
-
-
-def gather_blocks(own_enc, own_ffn, own_proj, own_dec, depth):
+
+    def finish():
+        for level in levels:
+            drain(level)
+
+    return step_action, finish
+
+
+def gather_encode_kernel(depth, batch, own_enc, own_ffn, own_proj, own_dec, pick, patches, vec, up_bias, pos,
+                         ffn, proj, dec, wide_out, *rest):
+    outs, rest = rest[:11], rest[11:]
+    blocks, wide, ffn_here = rest[:3]
+    held = rest[3:14]
+    kept, start, normed, qkv, mixed, middle, normed_two, slope, active, output, latent = held
+    first_sems, second_sems, local, load_sem, wide_sem, out_sems = rest[14:26], rest[26:38], *rest[38:]
+    row = lax.axis_index("row")
+    col = lax.axis_index("col")
+    y, x, z, k = row // 2, row % 2, col // 2, col % 2
+    row_x = y * 2 + (1 - x)
+    row_y = (1 - y) * 2 + x
+    row_d = (1 - y) * 2 + (1 - x)
+    near_x, near_y = (row_x, col), (row_y, col)
+    twin = (row, z * 2 + (1 - k))
+    lower, upper = (row, col - 2), (row, col + 2)
+    has_lower, has_upper = z > 0, z < depth - 1
+
+    barrier = pltpu.get_barrier_semaphore()
+    for other in (near_x, near_y, twin):
+        pl.semaphore_signal(barrier, inc=1, device_id=other, device_id_type=MESH)
+
+    @pl.when(has_lower)
+    def _():
+        pl.semaphore_signal(barrier, inc=1, device_id=lower, device_id_type=MESH)
+
+    @pl.when(has_upper)
+    def _():
+        pl.semaphore_signal(barrier, inc=1, device_id=upper, device_id_type=MESH)
+
+    pl.semaphore_wait(barrier, 3 + jnp.where(has_lower, 1, 0) + jnp.where(has_upper, 1, 0))
+    ids = (row, row_x, row_y, row_d, z, k, near_x, near_y, twin, lower, upper, has_lower, has_upper)
+    tall, short = own_enc.shape[0], own_dec.shape[1]
+    broad, thin = own_ffn.shape[2], own_dec.shape[2]
+
+    def rows_of(row_now, size, half):
+        part = size if half is None else size // 2
+        first = 0 if half is None else half * part
+        return pl.ds(pl.multiple_of(row_now * size + first, 16), part)
+
+    def cut_first(index, row_now, half=None):
+        rows = rows_of(row_now, tall, half)
+        return blocks.at[index, rows], ffn.at[:, rows, pl.ds(pl.multiple_of(index * broad, LANES), broad)]
+
+    def cut_second(index, row_now, half=None):
+        return (
+            proj.at[index, rows_of(row_now, tall, half)],
+            dec.at[:, rows_of(row_now, short, half), pl.ds(pl.multiple_of(index * thin, LANES), thin)],
+        )
+
+    own_first, own_second = (own_enc, own_ffn), (own_proj, own_dec)
+    step_first, finish_first = gather_steps(depth, ids, own_first, cut_first, first_sems)
+    step_second, finish_second = gather_steps(depth, ids, own_second, cut_second, second_sems)
+    keep = [
+        pltpu.make_async_copy(src, dst, local.at[item])
+        for item, (src, dst) in enumerate(
+            zip(own_first + own_second, cut_first(col, row) + cut_second(col, row))
+        )
+    ]
+    for item in keep:
+        item.start()
+    for step in range(depth + 1):
+        step_first(step)
+    step_second(0)
+    step_first(depth + 1)
+    finish_first()
+    for item in keep:
+        item.wait()
+    load = pltpu.make_async_copy(ffn, ffn_here, load_sem)
+    load.start()
+    count, _, width = blocks.shape
+
+    def assemble(first, last):
+        for index in range(first, last):
+            wide[:, index * width : (index + 1) * width] = blocks[index]
+
+    def flush(index):
+        return pltpu.make_async_copy(held[index], outs[index], out_sems.at[index])
+
+    assemble(0, count // 2)
+    step_second(1)
+    assemble(count // 2, count)
+    wide_copy = pltpu.make_async_copy(wide, wide_out, wide_sem)
+    wide_copy.start()
+    enc_embed(batch, pick, patches, wide, vec, pos, kept, start)
+    flush(0).start()
+    flush(1).start()
+    step_second(2)
+    enc_project(wide, vec, start, normed, qkv)
+    flush(2).start()
+    flush(3).start()
+    enc_mix(batch, qkv, mixed)
+    flush(4).start()
+    step_second(3)
+    enc_join(wide, vec, start, mixed, middle, normed_two)
+    flush(5).start()
+    flush(6).start()
+    load.wait()
+    total = middle[...] + vec[9:10]
+    source = normed_two[...]
+    step = 512
+    for place in range(0, F, step):
+        span = slice(place, place + step)
+        value, gain = gelu_pair(nn(source, ffn_here[0, :, span]) + up_bias[:, span])
+        slope[:, span] = gain
+        value = value.astype(low_type)
+        active[:, span] = value
+        total = total + nt(value, ffn_here[1, :, span])
+        if place == 2 * step:
+            step_second(4)
+    flush(7).start()
+    flush(8).start()
+    step_second(5)
+    output[...] = total
+    unit, _ = standard(total)
+    latent[...] = (unit * vec[10:11] + vec[11:12]).astype(low_type)
+    flush(9).start()
+    flush(10).start()
+    for step in range(6, depth + 2):
+        step_second(step)
+    finish_second()
+    wide_copy.wait()
+    for index in range(11):
+        flush(index).wait()
+
+
+def gather_encode(own_enc, own_ffn, own_proj, own_dec, depth, pick, padded, vec, up_bias):
     count = 2 * depth - 1
     cols = 2 * depth
     dma = pltpu.SemaphoreType.DMA
-    anywhere = pl.BlockSpec(memory_space=pltpu.HBM)
     tall, width = own_enc.shape
     shape = jax.ShapeDtypeStruct
     kind = own_enc.dtype
-    return pl.pallas_call(
-        functools.partial(gather_kernel, depth),
+    batch = padded.shape[0]
+    first, second = encoder_shapes(batch)
+    made = first + second
+    sems = [dma((count, 2, 2)), dma((depth, 2, 2))] + [dma((count, 2)) for _ in range(8)]
+    sems = sems + [dma((count, 4, 2)), dma((count, 4, 2))]
+    outs = pl.pallas_call(
+        functools.partial(gather_encode_kernel, depth, batch),
         out_shape=(
-            shape((cols, 4 * tall, width), kind),
             shape((2, 4 * tall, cols * own_ffn.shape[2]), kind),
             shape((cols, 4 * tall, own_proj.shape[1]), kind),
             shape((3, 4 * own_dec.shape[1], cols * own_dec.shape[2]), kind),
+            shape((D, 5 * D), kind),
+        )
+        + made,
+        in_specs=[hbm()] * 4 + [whole()] * 5,
+        out_specs=[hbm()] * 15,
+        scratch_shapes=[
+            pltpu.VMEM((cols, 4 * tall, width), kind),
+            pltpu.VMEM((D, 5 * D), kind),
+            pltpu.VMEM((2, D, F), kind),
+        ]
+        + [pltpu.VMEM(item.shape, item.dtype) for item in made]
+        + sems
+        + sems
+        + [dma((4,)), dma, dma, dma((11,))],
+        compiler_params=pltpu.CompilerParams(
+            collective_id=0, has_side_effects=True, vmem_limit_bytes=60 << 20
         ),
-        in_specs=[anywhere] * 4,
-        out_specs=[anywhere] * 4,
-        scratch_shapes=[dma((count, 2, 4)), dma((depth, 2, 4))]
-        + [dma((count, 4)) for _ in range(8)]
-        + [dma((count, 4, 4)), dma((count, 4, 4)), dma((4,))],
-        compiler_params=pltpu.CompilerParams(collective_id=0, has_side_effects=True),
-        name="gather_blocks",
-    )(own_enc, own_ffn, own_proj, own_dec)
+        name="gather_encode",
+    )(own_enc, own_ffn, own_proj, own_dec, pick, padded, vec, up_bias, jnp.asarray(table_of(D, DEC_ROWS)))
+    ffn, proj, dec, wide = outs[:4]
+    return ffn, proj, dec, wide, tuple(outs[4:])
 
 
 def far_first(depth):
@@ -480,7 +581,7 @@
         def _():
             out[span(t)] = arrived[t, row]
 
-    lags = (2, 4, 6)
+    lags = LAGS
 
     def body(i, carry):
         @pl.when(i + ahead < steps)
@@ -712,7 +813,7 @@
         wide[:, index * width : (index + 1) * width] = blocks[index]
 
 
-def enc_attend_kernel(batch, pick, patches, wide, vec, pos, kept, start, normed, qkv, mixed, middle, normed_two):
+def enc_embed(batch, pick, patches, wide, vec, pos, kept, start):
     rows = ENC_ROWS
     for image in range(batch):
         span = pl.ds(image * rows, rows)
@@ -725,6 +826,9 @@
         placed = nn(picks, parts[0]) + nn(picks, parts[1]) + nn(picks, parts[2])
         inner = lax.broadcasted_iota(jnp.int32, placed.shape, 0)
         start[span] = jnp.where(inner == CLASS_ENC, vec[1:2], start[span] + placed)
+
+
+def enc_project(wide, vec, start, normed, qkv):
     unit, _ = standard(start[...])
     normed[...] = (unit * vec[2:3] + vec[3:4]).astype(low_type)
     scale = 1.0 / math.sqrt(D // HE)
@@ -732,6 +836,10 @@
     qkv[:, :D] = ((nn(rows_in, wide[:, D : 2 * D]) + vec[4:5]) * scale).astype(low_type)
     qkv[:, D : 2 * D] = nn(rows_in, wide[:, 2 * D : 3 * D]).astype(low_type)
     qkv[:, 2 * D :] = (nn(rows_in, wide[:, 3 * D : 4 * D]) + vec[5:6]).astype(low_type)
+
+
+def enc_mix(batch, qkv, mixed):
+    rows = ENC_ROWS
     heads = LANES * HE // D
     for image in range(batch):
         span = pl.ds(image * rows, rows)
@@ -744,12 +852,22 @@
                 heads,
                 KEEP + 1,
             ).astype(low_type)
+
+
+def enc_join(wide, vec, start, mixed, middle, normed_two):
     middle[...] = start[...] + (nn(mixed[...], wide[:, 4 * D :]) + vec[6:7])
     unit, _ = standard(middle[...])
     normed_two[...] = (unit * vec[7:8] + vec[8:9]).astype(low_type)
 
 
-def enc_ffn_kernel(last, middle, normed_two, ffn, vec, up_bias, proj, dec_vec, slope, active, output, latent, entry):
+def enc_attend_kernel(batch, pick, patches, wide, vec, pos, kept, start, normed, qkv, mixed, middle, normed_two):
+    enc_embed(batch, pick, patches, wide, vec, pos, kept, start)
+    enc_project(wide, vec, start, normed, qkv)
+    enc_mix(batch, qkv, mixed)
+    enc_join(wide, vec, start, mixed, middle, normed_two)
+
+
+def enc_ffn_kernel(last, middle, normed_two, ffn, vec, up_bias, slope, active, output, latent):
     step = pl.program_id(0)
 
     @pl.when(step == 0)
@@ -765,15 +883,14 @@
     @pl.when(step == last)
     def _():
         unit, _ = standard(output[...])
-        rows = (unit * vec[10:11] + vec[11:12]).astype(low_type)
-        latent[...] = rows
-        entry[...] = nn(rows, proj[...]) + dec_vec[0:1]
-
-
-def dec_attend_kernel(entry, picked, pos, wide, vec, start, normed, qkv, mixed, middle, normed_two):
+        latent[...] = (unit * vec[10:11] + vec[11:12]).astype(low_type)
+
+
+def dec_attend_kernel(latent, proj, picked, pos, wide, vec, start, normed, qkv, mixed, middle, normed_two):
     picks = picked[0]
     kept = jnp.sum(picks.astype(high_type), 1, keepdims=True)
-    rows = place_rows(picks, entry[...]) + (1.0 - kept) * vec[1:2] + pos[...]
+    entry = nn(latent[...], proj[...]) + vec[0:1]
+    rows = place_rows(picks, entry) + (1.0 - kept) * vec[1:2] + pos[...]
     start[...] = rows
     unit, _ = standard(rows)
     rows_in = (unit * vec[2:3] + vec[3:4]).astype(low_type)
@@ -1141,11 +1258,8 @@
     return pltpu.CompilerParams(vmem_limit_bytes=60 << 20, **more)
 
 
-def local_grads(enc_blocks, enc_ffn, proj, dec3, head_low, smalls_parts, patches, shuffle, count):
-    enc_vec, enc_up, dec_vec, dec_up, head_bias = smalls_parts
-    enc_up, dec_up, head_bias = enc_up[None], dec_up[None], head_bias[None]
-    batch = patches.shape[0]
-    shape = jax.ShapeDtypeStruct
+def picks_of(shuffle):
+    batch = shuffle.shape[0]
     keep = jnp.concatenate(
         [
             shuffle[:, :KEEP],
@@ -1157,72 +1271,91 @@
     places = jnp.arange(DEC_ROWS, dtype=jnp.int32)
     pick = (keep[:, :, None] == places[None, None, :]).astype(low_type)
     picked = (keep[:, None, :] == places[None, :, None]).astype(low_type)
-    padded = jnp.pad(patches, ((0, 0), (0, DEC_ROWS - PATCHES), (0, 0)))
-    enc_pos = jnp.asarray(table_of(D, DEC_ROWS))
-    dec_pos = jnp.asarray(table_of(E, DEC_ROWS))
-    rows, dec_rows = batch * ENC_ROWS, batch * DEC_ROWS
-
+    return pick, picked
+
+
+def by_image(*block):
+    return pl.BlockSpec(block, lambda i: (i,) + (0,) * (len(block) - 1))
+
+
+def fixed(*block):
+    return pl.BlockSpec(block, lambda i: (0,) * len(block))
+
+
+def encoder_shapes(batch):
+    rows = batch * ENC_ROWS
+    shape = jax.ShapeDtypeStruct
+    first = (
+        shape((rows, D), low_type),
+        shape((rows, D), high_type),
+        shape((rows, D), low_type),
+        shape((rows, 3 * D), low_type),
+        shape((rows, D), low_type),
+        shape((rows, D), high_type),
+        shape((rows, D), low_type),
+    )
+    second = (
+        shape((rows, F), high_type),
+        shape((rows, F), low_type),
+        shape((rows, D), high_type),
+        shape((rows, D), low_type),
+    )
+    return first, second
+
+
+def encode_images(enc_blocks, enc_ffn, enc_vec, enc_up, pick, padded):
+    batch = padded.shape[0]
+    rows = batch * ENC_ROWS
+    first, second = encoder_shapes(batch)
     wide = pl.pallas_call(
         wide_kernel,
-        out_shape=shape((D, 5 * D), low_type),
+        out_shape=jax.ShapeDtypeStruct((D, 5 * D), low_type),
         in_specs=[whole()],
         out_specs=whole(),
         compiler_params=params(),
         name="wide",
     )(enc_blocks)
-    kept, start, normed, qkv, mixed, middle, normed_two = pl.pallas_call(
+    early = pl.pallas_call(
         functools.partial(enc_attend_kernel, batch),
-        out_shape=(
-            shape((rows, D), low_type),
-            shape((rows, D), high_type),
-            shape((rows, D), low_type),
-            shape((rows, 3 * D), low_type),
-            shape((rows, D), low_type),
-            shape((rows, D), high_type),
-            shape((rows, D), low_type),
-        ),
+        out_shape=first,
         in_specs=[whole()] * 5,
         out_specs=[whole()] * 7,
         compiler_params=params(),
         name="enc_attend",
-    )(pick, padded, wide, enc_vec, enc_pos)
-    def by_image(*block):
-        return pl.BlockSpec(block, lambda i: (i,) + (0,) * (len(block) - 1))
-
-    def fixed(*block):
-        return pl.BlockSpec(block, lambda i: (0,) * len(block))
-
+    )(pick, padded, wide, enc_vec, jnp.asarray(table_of(D, DEC_ROWS)))
     chunk = 512
-    rows_whole = lambda width: fixed(rows, width)
-    slope, active, enc_out, latent, entry = pl.pallas_call(
+    late = pl.pallas_call(
         functools.partial(enc_ffn_kernel, F // chunk - 1),
         grid=(F // chunk,),
-        out_shape=(
-            shape((rows, F), high_type),
-            shape((rows, F), low_type),
-            shape((rows, D), high_type),
-            shape((rows, D), low_type),
-            shape((rows, E), high_type),
-        ),
+        out_shape=second,
         in_specs=[
-            rows_whole(D),
-            rows_whole(D),
+            fixed(rows, D),
+            fixed(rows, D),
             pl.BlockSpec((2, D, chunk), lambda i: (0, 0, i)),
             fixed(12, D),
             pl.BlockSpec((1, chunk), lambda i: (0, i)),
-            fixed(D, E),
-            fixed(12, E),
         ],
         out_specs=[
             pl.BlockSpec((rows, chunk), lambda i: (0, i)),
             pl.BlockSpec((rows, chunk), lambda i: (0, i)),
-            rows_whole(D),
-            rows_whole(D),
-            rows_whole(E),
+            fixed(rows, D),
+            fixed(rows, D),
         ],
         compiler_params=params(),
         name="enc_ffn",
-    )(middle, normed_two, enc_ffn, enc_vec, enc_up, proj, dec_vec)
+    )(early[5], early[6], enc_ffn, enc_vec, enc_up)
+    return wide, early + tuple(late)
+
+
+def local_grads(wide, enc_ffn, proj, dec3, encoded, head_low, smalls_parts, pick, picked, padded, count):
+    enc_vec, _, dec_vec, dec_up, head_bias = smalls_parts
+    dec_up, head_bias = dec_up[None], head_bias[None]
+    kept, start, normed, qkv, mixed, middle, normed_two, slope, active, enc_out, latent = encoded
+    batch = padded.shape[0]
+    shape = jax.ShapeDtypeStruct
+    dec_pos = jnp.asarray(table_of(E, DEC_ROWS))
+    rows, dec_rows = batch * ENC_ROWS, batch * DEC_ROWS
+    chunk = 512
 
     dec_start, dec_normed, dec_qkv, dec_mixed, dec_middle, dec_normed_two = pl.pallas_call(
         dec_attend_kernel,
@@ -1236,7 +1369,8 @@
             shape((dec_rows, E), low_type),
         ),
         in_specs=[
-            by_image(ENC_ROWS, E),
+            by_image(ENC_ROWS, D),
+            fixed(D, E),
             by_image(1, DEC_ROWS, ENC_ROWS),
             fixed(DEC_ROWS, E),
             fixed(1, E, 4 * E),
@@ -1252,7 +1386,7 @@
         ],
         compiler_params=params(),
         name="dec_attend",
-    )(entry, picked, dec_pos, dec3, dec_vec)
+    )(latent, proj, picked, dec_pos, dec3, dec_vec)
 
     images = 2 if batch % 2 == 0 else 1
     block = images * DEC_ROWS
@@ -1341,11 +1475,11 @@
         ),
         in_specs=[
             hbm(),
-            rows_whole(E),
-            rows_whole(D),
-            rows_whole(D),
-            rows_whole(D),
-            rows_whole(D),
+            fixed(rows, E),
+            fixed(rows, D),
+            fixed(rows, D),
+            fixed(rows, D),
+            fixed(rows, D),
             pl.BlockSpec((rows, chunk), lambda i: (0, i)),
             pl.BlockSpec((rows, chunk), lambda i: (0, i)),
             pl.BlockSpec((2, D, chunk), lambda i: (0, 0, i)),
@@ -1353,7 +1487,7 @@
             fixed(12, D),
         ],
         out_specs=[
-            rows_whole(D),
+            fixed(rows, D),
             fixed(12, D),
             pl.BlockSpec((1, chunk), lambda i: (0, i)),
             fixed(1, E),
@@ -1440,16 +1574,20 @@
     return lax.axis_size("row") == 4 and lax.axis_size("col") == 8
 
 
-def gather_weights(enc_w, enc_ffn, dec_proj, dec_w, dec_ffn):
+def gather_and_encode(enc_w, enc_ffn, dec_proj, dec_w, dec_ffn, enc_vec, enc_up, pick, padded):
     shards = [item.astype(low_type) for item in (enc_w, enc_ffn, dec_proj, jnp.concatenate([dec_w[None], dec_ffn], 0))]
     if on_small_plane():
-        enc, ffn, proj, dec = gather_blocks(*shards, lax.axis_size("col") // 2)
-        return enc, ffn, proj.transpose(1, 0, 2).reshape(D, E), dec
+        ffn, proj, dec, wide, encoded = gather_encode(
+            *shards, lax.axis_size("col") // 2, pick, padded, enc_vec, enc_up[None]
+        )
+        return wide, ffn, proj.transpose(1, 0, 2).reshape(D, E), dec, encoded
     full = []
     for item in shards:
         rowed = lax.all_gather(item, "row", axis=item.ndim - 2, tiled=True)
         full.append(lax.all_gather(rowed, "col", axis=item.ndim - 1, tiled=True))
-    return full[0].reshape(D, 8, 5 * D // 8).transpose(1, 0, 2), full[1], full[2], full[3]
+    blocks = full[0].reshape(D, 8, 5 * D // 8).transpose(1, 0, 2)
+    wide, encoded = encode_images(blocks, full[1], enc_vec, enc_up[None], pick, padded)
+    return wide, full[1], full[2], full[3], encoded
 
 
 def apply_updates(blob, grad_head, smalls, loss, params_now, firsts, seconds):
@@ -1507,10 +1645,15 @@
     second_head_w,
     second_smalls,
 ):
-    enc_blocks, enc_ffn_w, proj, dec3 = gather_weights(enc_w, enc_ffn, dec_proj, dec_w, dec_ffn)
+    pick, picked = picks_of(shuffle)
+    padded = jnp.pad(patches, ((0, 0), (0, DEC_ROWS - PATCHES), (0, 0)))
+    parts = unpack(smalls)
+    wide, ffn, proj, dec, encoded = gather_and_encode(
+        enc_w, enc_ffn, dec_proj, dec_w, dec_ffn, parts[0], parts[1], pick, padded
+    )
     count = patches.shape[0] * lax.axis_size("row") * lax.axis_size("col") * (PATCHES - KEEP) * P_SIZE
     blob, grad_head, grad_smalls, loss_local = local_grads(
-        enc_blocks, enc_ffn_w, proj, dec3, head_w.astype(low_type), unpack(smalls), patches, shuffle, count
+        wide, ffn, proj, dec, encoded, head_w.astype(low_type), parts, pick, picked, padded, count
     )
     params_now = (enc_w, enc_ffn, dec_proj, dec_w, dec_ffn, head_w, smalls)
     firsts = (

time: 464 us -> 445 us (0.959)
  Pallas kernels: 410 us -> 389 us
    pallas_call x4 -> x1, Pallas kernels: 142 us -> 116 us  [gather_encode(): pl.pallas_call(functools.partial(gather_encode_kernel, depth, batch), out...]
  transfers between devices with their start and end apart: 1 -> 1, of which waited for: 0 -> 0; matrix products, arithmetic and copies ran while one was open for 2% -> 2% of each run, Pallas kernels for 41% -> 44%
where the time goes in v1:
time: 445 us; the launch traced here: 438 us
  Pallas kernels  389 us (87%)
  local copies, waits for them, and re-layouts  24.6 us (6%)
  between operations  16.3 us (4%)
  other arithmetic  8.26 us (2%)
    pallas_call x1, Pallas kernels, reduce_blocks(): pl.pallas_call(functools.partial(reduce_kernel, depth, devices, cols, par...  124 us
    pallas_call x1, Pallas kernels, gather_encode(): pl.pallas_call(functools.partial(gather_encode_kernel, depth, batch), out...  116 us
    pallas_call x1, Pallas kernels, local_grads(): pl.pallas_call(functools.partial(dec_ffn_kernel, images, batch // images...  47.2 us
    pallas_call x1, Pallas kernels, local_grads(): pl.pallas_call(functools.partial(dec_back_kernel, batch - 1), grid=(batch...  29.9 us
    pallas_call x1, Pallas kernels, local_grads(): pl.pallas_call(dec_attend_kernel, grid=(batch,), out_shape=(shape((dec_ro...  23.6 us
    pallas_call x1, Pallas kernels, local_grads(): pl.pallas_call(functools.partial(enc_ffn_back_kernel, F // chunk - 1), gr...  21 us
    pallas_call x1, Pallas kernels, local_grads(): pl.pallas_call(functools.partial(enc_back_kernel, batch), out_shape=(shap...  16.2 us
    pallas_call x1, Pallas kernels, apply_updates(): pl.pallas_call(adam_kernel, out_shape=tuple((jax.ShapeDtypeStruct(item.sh...  10.9 us
  transfers between devices with their start and end apart: 1, of which 0 were waited for; matrix products, arithmetic and copies ran while one was open for 2% of the time, Pallas kernels for 44%

profile of v1, /device:TPU:0, one launch (start us, length us, event | category | flops | bytes accessed | tf_op | source)
XLA Modules:
  0.0 438.1 jit_solution(695605960369557599)
XLA Ops:
  7.3 0.9 slice.43
  8.2 1.3 slice.44
  12.0 1.3 slice.46
  13.9 1.0 convert.8
  14.8 0.9 convert_bitcast_fusion
  18.0 1.4 pad.6.patches
  20.1 116.5 %gather_encode.1 = (bf16[2,768,3072]{2,1,0:T(8,128)(2,1)}, bf16[8,768,64]{2,1,0:T(8,128)(2,1)}, bf16[3,512,2048]{2,1,0:T(8,128)(2,1)}, bf16[768,3840]{1,0:T(8,12...) custom-call(bf16[192,480]{1,0:T(8,128)(2,1)} %convert_element_type.2, ...), custom_call_target="tpu_custom_call" | custom-call | tf_op jit(solution)/shard_map/gather_encode/pallas_call | solution.py:349
  136.6 1.8 copy.69
  138.4 1.2 copy.70.proj
  140.2 1.0 convert_element_type.26.head
  141.8 23.6 %dec_attend.1 = (f32[1248,512]{1,0:T(8,128)}, bf16[1248,512]{1,0:T(8,128)(2,1)}, bf16[1248,1536]{1,0:T(8,128)(2,1)}, bf16[1248,512]{1,0:T(8,128)(2,1)}, f32[1248,512]{1,0:T(8,128)}, /*index=5*/bf16[1248,512]{1,0:T(8,128)(2,1)}) custom-call(bf16[384,768]{1,0:T(8,128)(2,1)} %get-tuple-element.96.latent, bf16[768,512]{1,0:T(8,128)(2,1)} %copy.70.proj, ...), custom_call_target="tpu_custom_call" | custom-call | tf_op jit(solution)/shard_map/dec_attend/pallas_call | solution.py:1360
  165.4 47.2 %dec_ffn.1 = (f32[1248,512]{1,0:T(8,128)}, bf16[1248,512]{1,0:T(8,128)(2,1)}, f32[512,768]{1,0:T(8,128)}, f32[12,512]{1,0:T(8,128)}, f32[1,2048]{1,0:T(1,128)}, ...) custom-call(f32[1248,512]{1,0:T(8,128)} %get-tuple-element.99.middle, ...), custom_call_target="tpu_custom_call" | custom-call | tf_op jit(solution)/shard_map/dec_ffn/pallas_call | solution.py:1396
  213.4 29.9 %dec_back.1 = (bf16[384,512]{1,0:T(8,128)(2,1)}, f32[12,512]{1,0:T(8,128)}, f32[8,4,2784,128]{3,2,1,0:T(8,128)}) custom-call(f32[8,4,2784,128]{3,2,1,0:T(8,128)} %get-tuple-element.102.blob_in, bf16[1248,1536]{1,0:T(8,128)(2,1)} %get-tuple-element.103.qkv, bf16[1248,512]{1,0:T(8,128)(2,1)} %get-tuple-element.104.normed, ...), custom_call_target="tpu_custom_call", output_to_operand_aliasing={{2}: (0, {})} | custom-call | tf_op jit(solution)/shard_map/dec_back/pallas_call | solution.py:1443
  244.0 21.0 %enc_ffn_back.1 = (f32[384,768]{1,0:T(8,128)}, f32[12,768]{1,0:T(8,128)}, f32[1,3072]{1,0:T(1,128)}, f32[1,512]{1,0:T(1,128)}, f32[8,4,2784,128]{3,2,1,0:T(8,128)}) custom-call(f32[8,4,2784,128]{3,2,1,0:T(8,128)} %get-tuple-element.108.blob_in, bf16[384,512]{1,0:T(8,128)(2,1)} %get-tuple-element.109.grad_entry, ...), custom_call_target="tpu_custom_call", output_to_operand_aliasing={{4}: (0, {})} | custom-call | tf_op jit(solution)/shard_map/enc_ffn_back/pallas_call | solution.py:1466
  266.0 16.2 %enc_back.1 = (f32[12,768]{1,0:T(8,128)}, f32[8,4,2784,128]{3,2,1,0:T(8,128)}) custom-call(f32[8,4,2784,128]{3,2,1,0:T(8,128)} %get-tuple-element.116.blob_in, bf16[384,2304]{1,0:T(8,128)(2,1)} %get-tuple-element.117.qkv, bf16[384,768]{1,0:T(8,128)(2,1)} %get-tuple-element.118.kept, ...), custom_call_target="tpu_custom_call", output_to_operand_aliasing={{1}: (0, {})} | custom-call | tf_op jit(solution)/shard_map/enc_back/pallas_call | solution.py:1510
  283.0 1.2 slice.48
  284.2 1.4 concatenate.14
  285.6 123.7 %reduce_blocks.1 = (f32[2784,128]{1,0:T(8,128)}, f32[32,8,128]{2,1,0:T(8,128)}) custom-call(f32[8,4,2784,128]{3,2,1,0:T(8,128)} %get-tuple-element.124.blob, f32[32,8,128]{2,1,0:T(8,128)} %bitcast.23), custom_call_target="tpu_custom_call" | custom-call | tf_op jit(solution)/shard_map/reduce_blocks/pallas_call | solution.py:649
  409.3 1.5 slice.51.refs_2_
  410.8 1.2 slice.52
  414.2 10.9 %adam.1 = (f32[192,480]{1,0:T(8,128)}, f32[2,192,384]{2,1,0:T(8,128)}, f32[192,64]{1,0:T(8,128)}, f32[128,256]{1,0:T(8,128)}, f32[2,128,256]{2,1,0:T(8,128)}, /*...) custom-call(f32[2784,128]{1,0:T(8,128)} %get-tuple-element.134.refs_, ...), custom_call_target="tpu_custom_call" | custom-call | tf_op jit(solution)/shard_map/adam/pallas_call | solution.py:1602
  425.1 1.6 copy.75
  426.7 1.6 copy.76
  428.3 1.6 copy.77
  (56 shorter events, 12.0 us)
Async XLA Ops:
  7.2 8.6 %copy-start.1 = (f32[2,192,384]{2,1,0:T(8,128)S(1)}, f32[2,192,384]{2,1,0:T(8,128)}, u32[]{:S(2)}) copy-start(f32[2,192,384]{2,1,0:T(8,128)} %refs_4_.1) | copy-start | bytes 1769476
  7.2 9.3 %copy-start.3 = (f32[192,480]{1,0:T(8,128)S(1)}, f32[192,480]{1,0:T(8,128)}, u32[]{:S(2)}) copy-start(f32[192,480]{1,0:T(8,128)} %refs_3_.1) | copy-start | bytes 1105924
  7.2 10.0 %copy-start.4 = (f32[192,64]{0,1:T(8,128)S(1)}, f32[192,64]{0,1:T(8,128)}, u32[]{:S(2)}) copy-start(f32[192,64]{0,1:T(8,128)} %param.31) | copy-start | bytes 147460
  7.2 10.7 %copy-start.2 = (bf16[6,196,768]{2,1,0:T(8,128)(2,1)S(1)}, bf16[6,196,768]{2,1,0:T(8,128)(2,1)}, u32[]{:S(2)}) copy-start(bf16[6,196,768]{2,1,0:T(8,128)(2,1)} %param.27) | copy-start | bytes 5419012
  7.2 407.0 %all-reduce.3.cloned.1.call-start = ((), (), s32[]{:S(2)}) async-start(), calls=%async_computation | async-start | bytes 3145728 | tf_op jit(solution)/shard_map/psum | solution.py:1595
  136.6 3.0 slice-start
  136.6 3.6 copy-start
  139.6 1.7 slice-start.1
  213.4 29.9 %copy-start.8 = (f32[12,512]{1,0:T(8,128)S(1)}, f32[12,512]{1,0:T(8,128)}, u32[]{:S(2)}) copy-start(f32[12,512]{1,0:T(8,128)} %get-tuple-element.128) | copy-start | bytes 73732
  265.9 16.2 %copy-start.7 = (f32[12,768]{1,0:T(8,128)S(1)}, f32[12,768]{1,0:T(8,128)}, u32[]{:S(2)}) copy-start(f32[12,768]{1,0:T(8,128)} %get-tuple-element.125) | copy-start | bytes 110596
  265.9 18.2 %copy-start.11 = (f32[1,768]{1,0:T(1,128)S(1)}, f32[1,768]{1,0:T(1,128)}, u32[]{:S(2)}) copy-start(f32[1,768]{1,0:T(1,128)} %get-tuple-element.132) | copy-start | bytes 9220
  265.9 18.3 %copy-start.9 = (f32[1,3072]{1,0:T(1,128)S(1)}, f32[1,3072]{1,0:T(1,128)}, u32[]{:S(2)}) copy-start(f32[1,3072]{1,0:T(1,128)} %get-tuple-element.127) | copy-start | bytes 36868
  265.9 18.3 %copy-start.10 = (f32[1,2048]{1,0:T(1,128)S(1)}, f32[1,2048]{1,0:T(1,128)}, u32[]{:S(2)}) copy-start(f32[1,2048]{1,0:T(1,128)} %get-tuple-element.131) | copy-start | bytes 24580
  285.6 126.4 %copy-start.5 = (f32[192,64]{0,1:T(8,128)S(1)}, f32[192,64]{0,1:T(8,128)}, u32[]{:S(2)}) copy-start(f32[192,64]{0,1:T(8,128)} %param.38) | copy-start | bytes 147460
  285.6 127.2 %copy-start.6 = (f32[192,64]{0,1:T(8,128)S(1)}, f32[192,64]{0,1:T(8,128)}, u32[]{:S(2)}) copy-start(f32[192,64]{0,1:T(8,128)} %param.45) | copy-start | bytes 147460
Sparse Core Ops, SparseCore 0:
  212.7 136.1 all-reduce.2

commit v2 on v1

--- a/solution.py
+++ b/solution.py
@@ -25,20 +25,6 @@
 norm_eps = 1e-06
 low_type = jnp.bfloat16
 high_type = jnp.float32
-
-
-def unpack(smalls):
-    first = 12 * D
-    second = first + F
-    third = second + 12 * E
-    fourth = third + H
-    return (
-        smalls[:first].reshape(12, D),
-        smalls[first:second],
-        smalls[second:third].reshape(12, E),
-        smalls[third:fourth],
-        smalls[fourth:],
-    )
 
 
 MESH = pl.DeviceIdType.MESH
@@ -1208,9 +1194,9 @@
     return weight - 0.02 * (direction + decay * weight), first_new, second_new
 
 
-def adam_kernel(*refs):
+def adam_kernel(count, *refs):
     summed, head, small = refs[:3]
-    ins, outs = refs[3:24], refs[24:]
+    ins, outs, loss = refs[3:24], refs[24:45], refs[45]
 
     def update(index, place, grad, decay=0.05):
         for target, value in zip(
@@ -1227,10 +1213,86 @@
             update(index, place if lead is None else (lead,) + place, summed[base : base + tall, :size])
             base += tall
     folded = summed[base : base + 96]
-    update(2, (slice(0, 96),), folded[:, :64])
-    update(2, (slice(96, 192),), folded[:, 64:])
+    turned = jnp.concatenate([folded, jnp.zeros((32, LANES), high_type)], 0).T
+    update(2, (slice(None), slice(0, 96)), turned[:64, :96])
+    update(2, (slice(None), slice(96, 192)), turned[64:, :96])
     update(5, (slice(None),), head[...])
-    update(6, (slice(None),), small[...], 0.0)
+    tall = ins[6].shape[0]
+    update(6, (slice(None),), small[:tall], 0.0)
+    loss[...] = small[tall : tall + 1, :1] / count
+
+
+SMALL_ROWS = 256
+SMALL_PARTS = ((12, D), (1, F), (12, E), (1, H), (1, P_SIZE))
+
+
+def prepare_kernel(enc_w, enc_ffn, proj_turned, dec_w, dec_ffn, head, smalls, shuffle, patches,
+                   own_enc, own_ffn, own_proj, own_dec, head_low, enc_vec, enc_up, dec_vec, dec_up, head_bias,
+                   pick, picked, padded):
+    own_enc[...] = enc_w[...].astype(low_type)
+    own_ffn[...] = enc_ffn[...].astype(low_type)
+    own_proj[...] = proj_turned[...].T.astype(low_type)
+    own_dec[0] = dec_w[...].astype(low_type)
+    own_dec[1] = dec_ffn[0].astype(low_type)
+    own_dec[2] = dec_ffn[1].astype(low_type)
+    head_low[...] = head[...].astype(low_type)
+    place = 0
+    for target in (enc_vec, enc_up, dec_vec, dec_up, head_bias):
+        for index in range(target.shape[0]):
+            for lane in range(0, target.shape[1], LANES):
+                target[index : index + 1, lane : lane + LANES] = smalls[place : place + 1]
+                place += 1
+    slot = lax.broadcasted_iota(jnp.int32, (DEC_ROWS, ENC_ROWS), 0)
+    order = lax.broadcasted_iota(jnp.int32, (DEC_ROWS, ENC_ROWS), 1)
+    for image in range(patches.shape[0]):
+        keep = jnp.where(order < KEEP, shuffle[image : image + 1, :ENC_ROWS], jnp.where(order == CLASS_ENC, CLASS_DEC, -1))
+        chosen = jnp.where(keep == slot, 1.0, 0.0)
+        picked[image] = chosen.astype(low_type)
+        pick[image] = chosen.T.astype(low_type)
+        padded[image, DEC_ROWS - 16 :] = jnp.zeros((16, P_SIZE), low_type)
+        padded[image, :PATCHES] = patches[image]
+
+
+def prepare(enc_w, enc_ffn, dec_proj, dec_w, dec_ffn, head, smalls, shuffle, patches):
+    batch = patches.shape[0]
+    shape = jax.ShapeDtypeStruct
+    outs = [shape(item.shape, low_type) for item in (enc_w, enc_ffn, dec_proj)]
+    outs += [shape((3,) + dec_w.shape, low_type), shape(head.shape, low_type)]
+    outs += [shape(item, high_type) for item in SMALL_PARTS]
+    outs += [
+        shape((batch, ENC_ROWS, DEC_ROWS), low_type),
+        shape((batch, DEC_ROWS, ENC_ROWS), low_type),
+        shape((batch, DEC_ROWS, P_SIZE), low_type),
+    ]
+    return pl.pallas_call(
+        prepare_kernel,
+        out_shape=tuple(outs),
+        in_specs=[whole()] * 9,
+        out_specs=[whole()] * 13,
+        compiler_params=params(),
+        name="prepare",
+    )(enc_w, enc_ffn, dec_proj.T, dec_w, dec_ffn, head, smalls.reshape(-1, LANES), shuffle, patches)
+
+
+def pack_kernel(enc_one, enc_two, enc_up, dec_one, dec_two, entry, dec_up, head_bias, loss, small):
+    place = 0
+
+    def put(value):
+        nonlocal place
+        for index in range(value.shape[0]):
+            for lane in range(0, value.shape[1], LANES):
+                small[place : place + 1] = value[index : index + 1, lane : lane + LANES]
+                place += 1
+
+    put(enc_one[...] + enc_two[...])
+    put(enc_up[...])
+    put(entry[...])
+    put(dec_one[1:] + dec_two[1:])
+    put(dec_up[...])
+    put(head_bias[...])
+    small[place : place + 1] = loss[:1]
+    place += 1
+    small[place:] = jnp.zeros((SMALL_ROWS - place, LANES), high_type)
 
 
 def table_of(width, rows):
@@ -1256,22 +1318,6 @@
 
 def params(**more):
     return pltpu.CompilerParams(vmem_limit_bytes=60 << 20, **more)
-
-
-def picks_of(shuffle):
-    batch = shuffle.shape[0]
-    keep = jnp.concatenate(
-        [
-            shuffle[:, :KEEP],
-            jnp.full((batch, 1), CLASS_DEC, jnp.int32),
-            jnp.full((batch, ENC_ROWS - KEEP - 1), -1, jnp.int32),
-        ],
-        1,
-    )
-    places = jnp.arange(DEC_ROWS, dtype=jnp.int32)
-    pick = (keep[:, :, None] == places[None, None, :]).astype(low_type)
-    picked = (keep[:, None, :] == places[None, :, None]).astype(low_type)
-    return pick, picked
 
 
 def by_image(*block):
@@ -1347,9 +1393,8 @@
     return wide, early + tuple(late)
 
 
-def local_grads(wide, enc_ffn, proj, dec3, encoded, head_low, smalls_parts, pick, picked, padded, count):
-    enc_vec, _, dec_vec, dec_up, head_bias = smalls_parts
-    dec_up, head_bias = dec_up[None], head_bias[None]
+def local_grads(wide, enc_ffn, proj, dec3, encoded, head_low, vectors, pick, picked, padded, count):
+    enc_vec, _, dec_vec, dec_up, head_bias = vectors
     kept, start, normed, qkv, mixed, middle, normed_two, slope, active, enc_out, latent = encoded
     batch = padded.shape[0]
     shape = jax.ShapeDtypeStruct
@@ -1522,17 +1567,15 @@
         compiler_params=params(),
         name="enc_back",
     )(blob, qkv, kept, normed, start, mixed, enc_grad_middle, wide, enc_vec)
-    dec_grad = (dec_grad_one + dec_grad_two).at[0].set(entry_grad[0])
-    smalls = jnp.concatenate(
-        [
-            (enc_grad_one + enc_grad_two).reshape(-1),
-            enc_up_grad[0],
-            dec_grad.reshape(-1),
-            dec_up_grad[0],
-            head_bias_grad[0],
-        ]
-    )
-    return blob, grad_head, smalls, loss[0, 0]
+    small = pl.pallas_call(
+        pack_kernel,
+        out_shape=shape((SMALL_ROWS, LANES), high_type),
+        in_specs=[whole()] * 9,
+        out_specs=whole(),
+        compiler_params=params(),
+        name="pack",
+    )(enc_grad_one, enc_grad_two, enc_up_grad, dec_grad_one, dec_grad_two, entry_grad, dec_up_grad, head_bias_grad, loss)
+    return blob, grad_head, small
 
 
 def untile(block, rows, width):
@@ -1574,11 +1617,10 @@
     return lax.axis_size("row") == 4 and lax.axis_size("col") == 8
 
 
-def gather_and_encode(enc_w, enc_ffn, dec_proj, dec_w, dec_ffn, enc_vec, enc_up, pick, padded):
-    shards = [item.astype(low_type) for item in (enc_w, enc_ffn, dec_proj, jnp.concatenate([dec_w[None], dec_ffn], 0))]
+def gather_and_encode(shards, enc_vec, enc_up, pick, padded):
     if on_small_plane():
         ffn, proj, dec, wide, encoded = gather_encode(
-            *shards, lax.axis_size("col") // 2, pick, padded, enc_vec, enc_up[None]
+            *shards, lax.axis_size("col") // 2, pick, padded, enc_vec, enc_up
         )
         return wide, ffn, proj.transpose(1, 0, 2).reshape(D, E), dec, encoded
     full = []
@@ -1586,38 +1628,37 @@
         rowed = lax.all_gather(item, "row", axis=item.ndim - 2, tiled=True)
         full.append(lax.all_gather(rowed, "col", axis=item.ndim - 1, tiled=True))
     blocks = full[0].reshape(D, 8, 5 * D // 8).transpose(1, 0, 2)
-    wide, encoded = encode_images(blocks, full[1], enc_vec, enc_up[None], pick, padded)
+    wide, encoded = encode_images(blocks, full[1], enc_vec, enc_up, pick, padded)
     return wide, full[1], full[2], full[3], encoded
 
 
-def apply_updates(blob, grad_head, smalls, loss, params_now, firsts, seconds):
-    count = smalls.shape[0]
+def apply_updates(blob, grad_head, small, count, params_now, firsts, seconds):
     summed_head = lax.psum(grad_head, ("row", "col"))
     if on_small_plane():
-        small = jnp.concatenate([smalls, loss[None], jnp.zeros((32 * 8 * LANES - count - 1,), high_type)])
         summed, small = reduce_blocks(blob, small.reshape(32, 8, LANES), lax.axis_size("col") // 2, 6)
-        small = small.reshape(-1, LANES)
-        flat = lambda group: group[:6] + (group[6].reshape(-1, LANES),)
+        flat = lambda group: group[:2] + (group[2].T,) + group[3:6] + (group[6].reshape(-1, LANES),)
         ins = flat(params_now) + flat(firsts) + flat(seconds)
+        shape = jax.ShapeDtypeStruct
         outs = pl.pallas_call(
-            adam_kernel,
-            out_shape=tuple(jax.ShapeDtypeStruct(item.shape, high_type) for item in ins),
+            functools.partial(adam_kernel, count),
+            out_shape=tuple(shape(item.shape, high_type) for item in ins) + (shape((1, 1), high_type),),
             in_specs=[whole()] * 24,
-            out_specs=[whole()] * 21,
+            out_specs=[whole()] * 22,
             compiler_params=params(),
             name="adam",
-        )(summed, summed_head, small[: count // LANES], *ins)
-        outs = [item.reshape(-1) if index % 7 == 6 else item for index, item in enumerate(outs)]
-        return outs, small[count // LANES, count % LANES]
+        )(summed, summed_head, small.reshape(SMALL_ROWS, LANES), *ins)
+        back = {2: lambda item: item.T, 6: lambda item: item.reshape(-1)}
+        return [back.get(index % 7, lambda item: item)(item) for index, item in enumerate(outs[:21])], outs[21].reshape(())
     shards = []
     for item in whole_arrays(blob):
         done = lax.psum_scatter(item, "col", scatter_dimension=item.ndim - 1, tiled=True)
         shards.append(lax.psum_scatter(done, "row", scatter_dimension=item.ndim - 2, tiled=True))
-    smalls, loss = lax.psum((smalls, loss), ("row", "col"))
-    grads = tuple(shards) + (summed_head, smalls)
+    small = lax.psum(small, ("row", "col")).reshape(-1)
+    size = params_now[6].shape[0]
+    grads = tuple(shards) + (summed_head, small[:size])
     decays = (0.05,) * 6 + (0.0,)
     results = [adam_parts(*item) for item in zip(params_now, grads, firsts, seconds, decays)]
-    return [item[kind] for kind in range(3) for item in results], loss
+    return [item[kind] for kind in range(3) for item in results], small[size] / count
 
 
 def body(
@@ -1645,15 +1686,12 @@
     second_head_w,
     second_smalls,
 ):
-    pick, picked = picks_of(shuffle)
-    padded = jnp.pad(patches, ((0, 0), (0, DEC_ROWS - PATCHES), (0, 0)))
-    parts = unpack(smalls)
-    wide, ffn, proj, dec, encoded = gather_and_encode(
-        enc_w, enc_ffn, dec_proj, dec_w, dec_ffn, parts[0], parts[1], pick, padded
-    )
+    prepared = prepare(enc_w, enc_ffn, dec_proj, dec_w, dec_ffn, head_w, smalls, shuffle, patches)
+    shards, head_low, vectors, (pick, picked, padded) = prepared[:4], prepared[4], prepared[5:10], prepared[10:]
+    wide, ffn, proj, dec, encoded = gather_and_encode(shards, vectors[0], vectors[1], pick, padded)
     count = patches.shape[0] * lax.axis_size("row") * lax.axis_size("col") * (PATCHES - KEEP) * P_SIZE
-    blob, grad_head, grad_smalls, loss_local = local_grads(
-        wide, ffn, proj, dec, encoded, head_w.astype(low_type), parts, pick, picked, padded, count
+    blob, grad_head, small = local_grads(
+        wide, ffn, proj, dec, encoded, head_low, vectors, pick, picked, padded, count
     )
     params_now = (enc_w, enc_ffn, dec_proj, dec_w, dec_ffn, head_w, smalls)
     firsts = (
@@ -1674,8 +1712,8 @@
         second_head_w,
         second_smalls,
     )
-    outs, loss_sum = apply_updates(blob, grad_head, grad_smalls, loss_local, params_now, firsts, seconds)
-    return tuple(outs) + (loss_sum / count,)
+    outs, loss = apply_updates(blob, grad_head, small, count, params_now, firsts, seconds)
+    return tuple(outs) + (loss,)
 
 
 def solution(mesh):

time: 445 us -> 419 us (0.942)
  local copies, waits for them, and re-layouts: 24.6 us -> 2.89 us
  other arithmetic: 8.26 us -> 0 us
  Pallas kernels: 389 us -> 395 us
    slice x11 -> x0, local copies, waits for them, and re-layouts: 8.14 us -> none  [the longest x1 1.53 us: apply_updates(): small[:count // LANES]]
    unnamed x30 -> x0, local copies, waits for them, and re-layouts: 7.1 us -> none
    pallas_call x1 -> x3, Pallas kernels: 10.9 us -> 17 us  [the longest x1 10.8 us: apply_updates(): pl.pallas_call(functools.partial(adam_kernel, count), out_shape=tuple((sh...]
  transfers between devices with their start and end apart: 1 -> 1, of which waited for: 0 -> 0; matrix products, arithmetic and copies ran while one was open for 2% -> 0% of each run, Pallas kernels for 44% -> 47%
where the time goes in v2:
time: 419 us; the launch traced here: 412 us
  Pallas kernels  395 us (94%)
  between operations  14.4 us (3%)
    pallas_call x1, Pallas kernels, reduce_blocks(): pl.pallas_call(functools.partial(reduce_kernel, depth, devices, cols, par...  124 us
    pallas_call x1, Pallas kernels, gather_encode(): pl.pallas_call(functools.partial(gather_encode_kernel, depth, batch), out...  116 us
    pallas_call x1, Pallas kernels, local_grads(): pl.pallas_call(functools.partial(dec_ffn_kernel, images, batch // images...  46.7 us
    pallas_call x1, Pallas kernels, local_grads(): pl.pallas_call(functools.partial(dec_back_kernel, batch - 1), grid=(batch...  30.3 us
    pallas_call x1, Pallas kernels, local_grads(): pl.pallas_call(dec_attend_kernel, grid=(batch,), out_shape=(shape((dec_ro...  23.6 us
    pallas_call x1, Pallas kernels, local_grads(): pl.pallas_call(functools.partial(enc_ffn_back_kernel, F // chunk - 1), gr...  21.1 us
    pallas_call x1, Pallas kernels, local_grads(): pl.pallas_call(functools.partial(enc_back_kernel, batch), out_shape=(shap...  16.2 us
    pallas_call x1, Pallas kernels, apply_updates(): pl.pallas_call(functools.partial(adam_kernel, count), out_shape=tuple((sh...  10.8 us
  transfers between devices with their start and end apart: 1, of which 0 were waited for; matrix products, arithmetic and copies ran while one was open for 0% of the time, Pallas kernels for 47%

profile of v2, /device:TPU:0, one launch (start us, length us, event | category | flops | bytes accessed | tf_op | source)
XLA Modules:
  0.0 412.5 jit_solution(15977987474934195390)
XLA Ops:
  7.2 0.0 all-reduce.2.cloned.1.call-start
  7.2 4.5 %prepare.1 = (bf16[192,480]{1,0:T(8,128)(2,1)}, bf16[2,192,384]{2,1,0:T(8,128)(2,1)}, bf16[192,64]{1,0:T(8,128)(2,1)}, bf16[3,128,256]{2,1,0:T(8,128)(2,1)}, bf1...) custom-call(f32[192,480]{1,0:T(8,128)} %refs_3_.1, ...), custom_call_target="tpu_custom_call" | custom-call | tf_op jit(solution)/shard_map/prepare/pallas_call | solution.py:1267
  11.8 116.5 %gather_encode.1 = (bf16[2,768,3072]{2,1,0:T(8,128)(2,1)}, bf16[8,768,64]{2,1,0:T(8,128)(2,1)}, bf16[3,512,2048]{2,1,0:T(8,128)(2,1)}, bf16[768,3840]{1,0:T(8,12...) custom-call(bf16[192,480]{1,0:T(8,128)(2,1)} %get-tuple-element.98.o, ...), custom_call_target="tpu_custom_call" | custom-call | tf_op jit(solution)/shard_map/gather_encode/pallas_call | solution.py:335
  128.3 1.7 copy.51
  130.0 1.2 copy.52.proj
  131.2 23.6 %dec_attend.1 = (f32[1248,512]{1,0:T(8,128)}, bf16[1248,512]{1,0:T(8,128)(2,1)}, bf16[1248,1536]{1,0:T(8,128)(2,1)}, bf16[1248,512]{1,0:T(8,128)(2,1)}, f32[1248,512]{1,0:T(8,128)}, /*index=5*/bf16[1248,512]{1,0:T(8,128)(2,1)}) custom-call(bf16[384,768]{1,0:T(8,128)(2,1)} %get-tuple-element.106.latent, bf16[768,512]{1,0:T(8,128)(2,1)} %copy.52.proj, ...), custom_call_target="tpu_custom_call" | custom-call | tf_op jit(solution)/shard_map/dec_attend/pallas_call | solution.py:1405
  154.8 46.7 %dec_ffn.3 = (f32[1248,512]{1,0:T(8,128)}, bf16[1248,512]{1,0:T(8,128)(2,1)}, f32[512,768]{1,0:T(8,128)}, f32[12,512]{1,0:T(8,128)}, f32[1,2048]{1,0:T(1,128)}, ...) custom-call(f32[1248,512]{1,0:T(8,128)} %get-tuple-element.111.middle, ...), custom_call_target="tpu_custom_call" | custom-call | tf_op jit(solution)/shard_map/dec_ffn/pallas_call | solution.py:1441
  201.5 0.0 all-reduce.2.cloned.1.call-update
  201.5 30.3 %dec_back.1 = (bf16[384,512]{1,0:T(8,128)(2,1)}, f32[12,512]{1,0:T(8,128)}, f32[8,4,2784,128]{3,2,1,0:T(8,128)}) custom-call(f32[8,4,2784,128]{3,2,1,0:T(8,128)} %get-tuple-element.117.blob_in, bf16[1248,1536]{1,0:T(8,128)(2,1)} %get-tuple-element.118.qkv, bf16[1248,512]{1,0:T(8,128)(2,1)} %get-tuple-element.119.normed, ...), custom_call_target="tpu_custom_call", output_to_operand_aliasing={{2}: (0, {})} | custom-call | tf_op jit(solution)/shard_map/dec_back/pallas_call | solution.py:1488
  231.8 21.1 %enc_ffn_back.1 = (f32[384,768]{1,0:T(8,128)}, f32[12,768]{1,0:T(8,128)}, f32[1,3072]{1,0:T(1,128)}, f32[1,512]{1,0:T(1,128)}, f32[8,4,2784,128]{3,2,1,0:T(8,128)}) custom-call(f32[8,4,2784,128]{3,2,1,0:T(8,128)} %get-tuple-element.123.blob_in, bf16[384,512]{1,0:T(8,128)(2,1)} %get-tuple-element.124.grad_entry, ...), custom_call_target="tpu_custom_call", output_to_operand_aliasing={{4}: (0, {})} | custom-call | tf_op jit(solution)/shard_map/enc_ffn_back/pallas_call | solution.py:1511
  252.9 16.2 %enc_back.1 = (f32[12,768]{1,0:T(8,128)}, f32[8,4,2784,128]{3,2,1,0:T(8,128)}) custom-call(f32[8,4,2784,128]{3,2,1,0:T(8,128)} %get-tuple-element.131.blob_in, bf16[384,2304]{1,0:T(8,128)(2,1)} %get-tuple-element.132.qkv, bf16[384,768]{1,0:T(8,128)(2,1)} %get-tuple-element.133.kept, ...), custom_call_target="tpu_custom_call", output_to_operand_aliasing={{1}: (0, {})} | custom-call | tf_op jit(solution)/shard_map/enc_back/pallas_call | solution.py:1555
  269.1 1.6 pack.1
  270.7 123.8 %reduce_blocks.1 = (f32[2784,128]{1,0:T(8,128)}, f32[32,8,128]{2,1,0:T(8,128)}) custom-call(f32[8,4,2784,128]{3,2,1,0:T(8,128)} %get-tuple-element.139.blob, f32[32,8,128]{2,1,0:T(8,128)} %bitcast.21), custom_call_target="tpu_custom_call" | custom-call | tf_op jit(solution)/shard_map/reduce_blocks/pallas_call | solution.py:635
  394.5 0.0 all-reduce.2.cloned.1.call-done.refs_1_
  394.6 10.8 %adam.1 = (f32[192,480]{1,0:T(8,128)}, f32[2,192,384]{2,1,0:T(8,128)}, f32[64,192]{1,0:T(8,128)}, f32[128,256]{1,0:T(8,128)}, f32[2,128,256]{2,1,0:T(8,128)}, /*...) custom-call(f32[2784,128]{1,0:T(8,128)} %get-tuple-element.149.refs_, ...), custom_call_target="tpu_custom_call" | custom-call | tf_op jit(solution)/shard_map/adam/pallas_call | solution.py:1642
Async XLA Ops:
  7.2 387.4 %all-reduce.2.cloned.1.call-start = ((), (), s32[]{:S(2)}) async-start(), calls=%async_computation | async-start | bytes 3145728 | tf_op jit(solution)/shard_map/psum | solution.py:1636
Sparse Core Ops, SparseCore 0:
  201.6 136.4 all-reduce.1

commit v3 on v2

--- a/solution.py
+++ b/solution.py
@@ -194,13 +194,129 @@
     return step_action, finish
 
 
+def gather_steps_late(depth, place_ids, own, cut, sems):
+    row, row_x, row_y, row_d, z, k, near_x, near_y, twin, lower, upper, has_lower, has_upper = place_ids
+    zs, zr, xs, xr, ys, yr, dxs, dxr, dys, dyr, cs, cr = sems
+    kinds = (row, row_x, row_y, row_d)
+    levels = [(0, 0)] + [(d, way) for d in range(1, depth) for way in (0, 1)]
+    level_of = {item: number for number, item in enumerate(levels)}
+
+    def refs(level, kind, half=None):
+        d, way = level
+        return cut((z - d if way == 0 else z + d) * 2 + k, kinds[kind], half)
+
+    def valid(level):
+        d, way = level
+        return z - d >= 0 if way == 0 else z + d < depth
+
+    def copy(src, dst, send, recv, target):
+        return Group(
+            [
+                pltpu.make_async_remote_copy(
+                    src_ref=src[item],
+                    dst_ref=dst[item],
+                    send_sem=send.at[item],
+                    recv_sem=recv.at[item],
+                    device_id=target,
+                    device_id_type=MESH,
+                )
+                for item in range(len(own))
+            ]
+        )
+
+    home = (0, 0)
+
+    def source(level, kind):
+        return own if level == home and kind == 0 else refs(level, kind)
+
+    def x_copy():
+        return copy(own, refs(home, 0), xs, xr, near_x)
+
+    def y_copy():
+        return copy(own, refs(home, 0), ys, yr, near_y)
+
+    def dx_copy():
+        return copy(refs(home, 2, 1), refs(home, 2, 1), dxs, dxr, near_x)
+
+    def dy_copy():
+        return copy(refs(home, 1, 0), refs(home, 1, 0), dys, dyr, near_y)
+
+    def z_copy(level, way, kind):
+        d = level[0]
+        target = upper if way == 0 else lower
+        return copy(source(level, kind), refs(level, kind), zs.at[d, way, kind], zr.at[d, way, kind], target)
+
+    def twin_copy(level, kind):
+        n = level_of[level]
+        return copy(source(level, kind), refs(level, kind), cs.at[n, kind], cr.at[n, kind], twin)
+
+    def outward(level, kind, action):
+        for way in (0, 1):
+            if (level == home or way == level[1]) and level[0] < depth - 1:
+                @pl.when(has_upper if way == 0 else has_lower)
+                def _():
+                    action(z_copy(level, way, kind))
+
+    def pass_on(level, kind):
+        outward(level, kind, lambda item: item.start())
+        twin_copy(level, kind).start()
+
+    def arrive(level, kind):
+        d, way = level
+
+        @pl.when(valid(level))
+        def _():
+            z_copy((d - 1, way if d > 1 else 0), way, kind).wait_recv()
+            pass_on(level, kind)
+
+    delay = (0, 1, 1, 2)
+
+    def step_action(step):
+        if step == 0:
+            x_copy().start()
+            y_copy().start()
+            pass_on(home, 0)
+        if step == 1:
+            x_copy().wait_recv()
+            dy_copy().start()
+            pass_on(home, 1)
+            y_copy().wait_recv()
+            dx_copy().start()
+            pass_on(home, 2)
+        if step == 2:
+            dx_copy().wait_recv()
+            dy_copy().wait_recv()
+            pass_on(home, 3)
+        for level in levels[1:]:
+            for kind in range(4):
+                if step == level[0] + delay[kind]:
+                    arrive(level, kind)
+
+    def finish():
+        for item in (x_copy(), y_copy(), dx_copy(), dy_copy()):
+            item.wait_send()
+        for level in levels:
+            def action():
+                for kind in range(4):
+                    outward(level, kind, lambda item: item.wait_send())
+                    twin_copy(level, kind).wait()
+
+            if level == home:
+                action()
+            else:
+                pl.when(valid(level))(action)
+
+    return step_action, finish
+
+
 def gather_encode_kernel(depth, batch, own_enc, own_ffn, own_proj, own_dec, pick, patches, vec, up_bias, pos,
                          ffn, proj, dec, wide_out, *rest):
     outs, rest = rest[:11], rest[11:]
     blocks, wide, ffn_here = rest[:3]
     held = rest[3:14]
     kept, start, normed, qkv, mixed, middle, normed_two, slope, active, output, latent = held
-    first_sems, second_sems, local, load_sem, wide_sem, out_sems = rest[14:26], rest[26:38], *rest[38:]
+    first_sems, second_sems, late_sems = rest[14:26], rest[26:38], rest[38:50]
+    local, load_sem, wide_sem, out_sems = rest[50:]
     row = lax.axis_index("row")
     col = lax.axis_index("col")
     y, x, z, k = row // 2, row % 2, col // 2, col % 2
@@ -229,14 +345,22 @@
     tall, short = own_enc.shape[0], own_dec.shape[1]
     broad, thin = own_ffn.shape[2], own_dec.shape[2]
 
-    def rows_of(row_now, size, half):
-        part = size if half is None else size // 2
-        first = 0 if half is None else half * part
+    early = tall - 32
+
+    def rows_of(row_now, size, half, start=0, count=None):
+        count = size if count is None else count
+        part = count if half is None else count // 2
+        first = start if half is None else start + half * part
         return pl.ds(pl.multiple_of(row_now * size + first, 16), part)
 
+    def enc_refs(index, rows):
+        return blocks.at[index, rows], ffn.at[:, rows, pl.ds(pl.multiple_of(index * broad, LANES), broad)]
+
     def cut_first(index, row_now, half=None):
-        rows = rows_of(row_now, tall, half)
-        return blocks.at[index, rows], ffn.at[:, rows, pl.ds(pl.multiple_of(index * broad, LANES), broad)]
+        return enc_refs(index, rows_of(row_now, tall, half, 0, early))
+
+    def cut_late(index, row_now, half=None):
+        return enc_refs(index, rows_of(row_now, tall, half, early, tall - early))
 
     def cut_second(index, row_now, half=None):
         return (
@@ -244,22 +368,28 @@
             dec.at[:, rows_of(row_now, short, half), pl.ds(pl.multiple_of(index * thin, LANES), thin)],
         )
 
-    own_first, own_second = (own_enc, own_ffn), (own_proj, own_dec)
+    own_second = (own_proj, own_dec)
+    own_first = (own_enc.at[pl.ds(0, early)], own_ffn.at[:, pl.ds(0, early)])
+    own_late = (own_enc.at[pl.ds(early, tall - early)], own_ffn.at[:, pl.ds(early, tall - early)])
     step_first, finish_first = gather_steps(depth, ids, own_first, cut_first, first_sems)
+    step_late, finish_late = gather_steps_late(depth, ids, own_late, cut_late, late_sems)
     step_second, finish_second = gather_steps(depth, ids, own_second, cut_second, second_sems)
     keep = [
         pltpu.make_async_copy(src, dst, local.at[item])
         for item, (src, dst) in enumerate(
-            zip(own_first + own_second, cut_first(col, row) + cut_second(col, row))
+            zip(own_first + own_late + own_second, cut_first(col, row) + cut_late(col, row) + cut_second(col, row))
         )
     ]
     for item in keep:
         item.start()
     for step in range(depth + 1):
         step_first(step)
+        step_late(step)
     step_second(0)
     step_first(depth + 1)
+    step_late(depth + 1)
     finish_first()
+    finish_late()
     for item in keep:
         item.wait()
     load = pltpu.make_async_copy(ffn, ffn_here, load_sem)
@@ -351,7 +481,10 @@
         + [pltpu.VMEM(item.shape, item.dtype) for item in made]
         + sems
         + sems
-        + [dma((4,)), dma, dma, dma((11,))],
+        + [dma((depth, 2, 4, 2)), dma((depth, 2, 4, 2))]
+        + [dma((2,)) for _ in range(8)]
+        + [dma((count, 4, 2)), dma((count, 4, 2))]
+        + [dma((6,)), dma, dma, dma((11,))],
         compiler_params=pltpu.CompilerParams(
             collective_id=0, has_side_effects=True, vmem_limit_bytes=60 << 20
         ),
@@ -965,17 +1098,30 @@
     grad_down = grad_out.astype(low_type)
     vec_grad[9:10] += col_sum(grad_down)
     grad_source = jnp.zeros_like(total)
+    grad_turned, source_turned = grad_down.T, source.T
     for place in range(0, H, wide):
         span = slice(place, place + wide)
         grad_up = (slope[:, span] * nn(grad_down, weights[2, :, span])).astype(low_type)
         up_grad[:, span] += col_sum(grad_up)
         grad_source = grad_source + nt(grad_up, weights[1, :, span])
-        piece = tn(grad_down, active[:, span])
-        other = tn(source, grad_up)
+        piece = nn(grad_turned, active[:, span])
+        other = nn(source_turned, grad_up)
         for tile in range(wide // LANES):
             lane = slice(tile * LANES, (tile + 1) * LANES)
             acc_down[place // LANES + tile] += piece[:, lane]
             acc_up[place // LANES + tile] += other[:, lane]
+
+        @pl.when(step == last)
+        def _():
+            tiles = wide // LANES
+            tile, block = place // LANES, place // LANES // 2
+            rows_block = E // 4
+            for number, (acc, base) in enumerate(((acc_up, 2176), (acc_down, 2432))):
+                send_tiles(
+                    acc.at[pl.ds(tile, tiles)], blob.at[pl.ds(block, tiles // 2)], sems.at[number], tiles,
+                    rows_block, 2, base, rows_block,
+                )
+
     unit, rate = standard(middle[...])
     vec_grad[7:8] += col_sum(grad_source * unit)
     vec_grad[8:9] += col_sum(grad_source)
@@ -991,8 +1137,6 @@
     @pl.when(step == last)
     def _():
         rows_block = E // 4
-        send_tiles(acc_up, blob, sems.at[0], H // LANES, rows_block, 2, 2176, rows_block)
-        send_tiles(acc_down, blob, sems.at[1], H // LANES, rows_block, 2, 2432, rows_block)
         send_tiles(acc_out, blob.at[pl.ds(6, 2)], sems.at[2], E // LANES, rows_block, 2, 1920, rows_block)
         wait_tiles(acc_up, sems.at[0])
         wait_tiles(acc_down, sems.at[1])
@@ -1026,9 +1170,9 @@
         grads[:, 2 * E + lane : 2 * E + lane + LANES] = value.astype(low_type)
     vec_grad[4:5] += col_sum(grads[:, :E])
     vec_grad[5:6] += col_sum(grads[:, 2 * E :])
-    rows = normed[...]
+    rows = normed[...].T
     for part in range(3):
-        piece = tn(rows, grads[:, part * E : (part + 1) * E])
+        piece = nn(rows, grads[:, part * E : (part + 1) * E])
         for tile in range(E // LANES):
             acc[part * (E // LANES) + tile] += piece[:, tile * LANES : (tile + 1) * LANES]
     grad_normed = nt(grads[...], weights[0, :, : 3 * E])
@@ -1049,7 +1193,7 @@
 
 def enc_ffn_back_kernel(last, blob_in, grad_entry, latent, output, middle, normed_two, slope, active, ffn, proj, vec,
                         grad_middle, vec_grad, up_grad, entry_grad, blob,
-                        grad_out, grad_down, grad_source, folded, acc_up, acc_down, fold_sem, sems):
+                        grad_out, grad_down, grad_turned, source_turned, grad_source, folded, acc_up, acc_down, fold_sem, sems):
     step = pl.program_id(0)
     fold_copy = pltpu.make_async_copy(folded, blob.at[:, :, pl.ds(2688, 96)], fold_sem)
     part_rows = D // 4
@@ -1075,6 +1219,8 @@
         rows = standard_back(unit, rate, grad_latent * vec[10:11])
         grad_out[...] = rows
         grad_down[...] = rows.astype(low_type)
+        grad_turned[...] = rows.T.astype(low_type)
+        source_turned[...] = normed_two[...].T
         vec_grad[9:10] = col_sum(rows.astype(low_type))
         grad_source[...] = jnp.zeros_like(grad_source)
 
@@ -1089,8 +1235,8 @@
     grad_up = (slope[...] * nn(grads, ffn[1])).astype(low_type)
     up_grad[...] = col_sum(grad_up)
     grad_source[...] += nt(grad_up, ffn[0])
-    piece = tn(grads, active[...])
-    other = tn(normed_two[...], grad_up)
+    piece = nn(grad_turned[...], active[...])
+    other = nn(source_turned[...], grad_up)
     count = grad_up.shape[1] // LANES
     for tile in range(count):
         lane = slice(tile * LANES, (tile + 1) * LANES)
@@ -1151,9 +1297,9 @@
         grads[:, 2 * D + lane : 2 * D + lane + LANES] = value.astype(low_type)
     vec_grad[4:5] = col_sum(grads[:, :D])
     vec_grad[5:6] = col_sum(grads[:, 2 * D :])
-    rows_in = normed[...]
+    rows_in = normed[...].T
     for part in range(3):
-        grad_wide[:, (part + 1) * D : (part + 2) * D] = tn(rows_in, grads[:, part * D : (part + 1) * D])
+        grad_wide[:, (part + 1) * D : (part + 2) * D] = nn(rows_in, grads[:, part * D : (part + 1) * D])
     width = 5 * D // 8
     tall = D // 4
 
@@ -1541,6 +1687,8 @@
         scratch_shapes=[
             vm((rows, D), high_type),
             vm((rows, D), low_type),
+            vm((D, rows), low_type),
+            vm((D, rows), low_type),
             vm((rows, D), high_type),
             vm((8, 4, 96, LANES), high_type),
             vm((2, chunk // LANES, D, LANES), high_type),

time: 419 us -> 418 us (level)
  transfers between devices with their start and end apart: 1 -> 1, of which waited for: 0 -> 0; matrix products, arithmetic and copies ran while one was open for 0% -> 0% of each run, Pallas kernels for 47% -> 46%
where the time goes in v3:
time: 418 us; the launch traced here: 411 us
  Pallas kernels  393 us (94%)
  between operations  14.3 us (3%)
    pallas_call x1, Pallas kernels, reduce_blocks(): pl.pallas_call(functools.partial(reduce_kernel, depth, devices, cols, par...  121 us
    pallas_call x1, Pallas kernels, gather_encode(): pl.pallas_call(functools.partial(gather_encode_kernel, depth, batch), out...  113 us
    pallas_call x1, Pallas kernels, local_grads(): pl.pallas_call(functools.partial(dec_ffn_kernel, images, batch // images...  50.2 us
    pallas_call x1, Pallas kernels, local_grads(): pl.pallas_call(functools.partial(dec_back_kernel, batch - 1), grid=(batch...  29.9 us
    pallas_call x1, Pallas kernels, local_grads(): pl.pallas_call(dec_attend_kernel, grid=(batch,), out_shape=(shape((dec_ro...  23.6 us
    pallas_call x1, Pallas kernels, local_grads(): pl.pallas_call(functools.partial(enc_ffn_back_kernel, F // chunk - 1), gr...  21.7 us
    pallas_call x1, Pallas kernels, local_grads(): pl.pallas_call(functools.partial(enc_back_kernel, batch), out_shape=(shap...  16.2 us
    pallas_call x1, Pallas kernels, apply_updates(): pl.pallas_call(functools.partial(adam_kernel, count), out_shape=tuple((sh...  10.8 us
  transfers between devices with their start and end apart: 1, of which 0 were waited for; matrix products, arithmetic and copies ran while one was open for 0% of the time, Pallas kernels for 46%

profile of v3, /device:TPU:0, one launch (start us, length us, event | category | flops | bytes accessed | tf_op | source)
XLA Modules:
  0.0 410.7 jit_solution(5405094541890318317)
XLA Ops:
  7.2 0.0 all-reduce.2.cloned.1.call-start
  7.2 4.5 %prepare.1 = (bf16[192,480]{1,0:T(8,128)(2,1)}, bf16[2,192,384]{2,1,0:T(8,128)(2,1)}, bf16[192,64]{1,0:T(8,128)(2,1)}, bf16[3,128,256]{2,1,0:T(8,128)(2,1)}, bf1...) custom-call(f32[192,480]{1,0:T(8,128)} %refs_3_.1, ...), custom_call_target="tpu_custom_call" | custom-call | tf_op jit(solution)/shard_map/prepare/pallas_call | solution.py:1413
  11.8 113.5 %gather_encode.1 = (bf16[2,768,3072]{2,1,0:T(8,128)(2,1)}, bf16[8,768,64]{2,1,0:T(8,128)(2,1)}, bf16[3,512,2048]{2,1,0:T(8,128)(2,1)}, bf16[768,3840]{1,0:T(8,12...) custom-call(bf16[192,480]{1,0:T(8,128)(2,1)} %get-tuple-element.98.o, ...), custom_call_target="tpu_custom_call" | custom-call | tf_op jit(solution)/shard_map/gather_encode/pallas_call | solution.py:465
  125.3 1.7 copy.51
  126.9 1.2 copy.52.proj
  128.2 23.6 %dec_attend.1 = (f32[1248,512]{1,0:T(8,128)}, bf16[1248,512]{1,0:T(8,128)(2,1)}, bf16[1248,1536]{1,0:T(8,128)(2,1)}, bf16[1248,512]{1,0:T(8,128)(2,1)}, f32[1248,512]{1,0:T(8,128)}, /*index=5*/bf16[1248,512]{1,0:T(8,128)(2,1)}) custom-call(bf16[384,768]{1,0:T(8,128)(2,1)} %get-tuple-element.106.latent, bf16[768,512]{1,0:T(8,128)(2,1)} %copy.52.proj, ...), custom_call_target="tpu_custom_call" | custom-call | tf_op jit(solution)/shard_map/dec_attend/pallas_call | solution.py:1551
  151.8 50.2 %dec_ffn.3 = (f32[1248,512]{1,0:T(8,128)}, bf16[1248,512]{1,0:T(8,128)(2,1)}, f32[512,768]{1,0:T(8,128)}, f32[12,512]{1,0:T(8,128)}, f32[1,2048]{1,0:T(1,128)}, ...) custom-call(f32[1248,512]{1,0:T(8,128)} %get-tuple-element.111.middle, ...), custom_call_target="tpu_custom_call" | custom-call | tf_op jit(solution)/shard_map/dec_ffn/pallas_call | solution.py:1587
  202.0 0.0 all-reduce.2.cloned.1.call-update
  202.0 29.9 %dec_back.1 = (bf16[384,512]{1,0:T(8,128)(2,1)}, f32[12,512]{1,0:T(8,128)}, f32[8,4,2784,128]{3,2,1,0:T(8,128)}) custom-call(f32[8,4,2784,128]{3,2,1,0:T(8,128)} %get-tuple-element.117.blob_in, bf16[1248,1536]{1,0:T(8,128)(2,1)} %get-tuple-element.118.qkv, bf16[1248,512]{1,0:T(8,128)(2,1)} %get-tuple-element.119.normed, ...), custom_call_target="tpu_custom_call", output_to_operand_aliasing={{2}: (0, {})} | custom-call | tf_op jit(solution)/shard_map/dec_back/pallas_call | solution.py:1634
  231.9 21.7 %enc_ffn_back.1 = (f32[384,768]{1,0:T(8,128)}, f32[12,768]{1,0:T(8,128)}, f32[1,3072]{1,0:T(1,128)}, f32[1,512]{1,0:T(1,128)}, f32[8,4,2784,128]{3,2,1,0:T(8,128)}) custom-call(f32[8,4,2784,128]{3,2,1,0:T(8,128)} %get-tuple-element.123.blob_in, bf16[384,512]{1,0:T(8,128)(2,1)} %get-tuple-element.124.grad_entry, ...), custom_call_target="tpu_custom_call", output_to_operand_aliasing={{4}: (0, {})} | custom-call | tf_op jit(solution)/shard_map/enc_ffn_back/pallas_call | solution.py:1657
  253.6 16.2 %enc_back.1 = (f32[12,768]{1,0:T(8,128)}, f32[8,4,2784,128]{3,2,1,0:T(8,128)}) custom-call(f32[8,4,2784,128]{3,2,1,0:T(8,128)} %get-tuple-element.131.blob_in, bf16[384,2304]{1,0:T(8,128)(2,1)} %get-tuple-element.132.qkv, bf16[384,768]{1,0:T(8,128)(2,1)} %get-tuple-element.133.kept, ...), custom_call_target="tpu_custom_call", output_to_operand_aliasing={{1}: (0, {})} | custom-call | tf_op jit(solution)/shard_map/enc_back/pallas_call | solution.py:1703
  269.8 1.6 pack.1
  271.3 121.4 %reduce_blocks.1 = (f32[2784,128]{1,0:T(8,128)}, f32[32,8,128]{2,1,0:T(8,128)}) custom-call(f32[8,4,2784,128]{3,2,1,0:T(8,128)} %get-tuple-element.139.blob, f32[32,8,128]{2,1,0:T(8,128)} %bitcast.21), custom_call_target="tpu_custom_call" | custom-call | tf_op jit(solution)/shard_map/reduce_blocks/pallas_call | solution.py:768
  392.8 0.0 all-reduce.2.cloned.1.call-done.refs_1_
  392.8 10.8 %adam.1 = (f32[192,480]{1,0:T(8,128)}, f32[2,192,384]{2,1,0:T(8,128)}, f32[64,192]{1,0:T(8,128)}, f32[128,256]{1,0:T(8,128)}, f32[2,128,256]{2,1,0:T(8,128)}, /*...) custom-call(f32[2784,128]{1,0:T(8,128)} %get-tuple-element.149.refs_, ...), custom_call_target="tpu_custom_call" | custom-call | tf_op jit(solution)/shard_map/adam/pallas_call | solution.py:1790
Async XLA Ops:
  7.2 385.6 %all-reduce.2.cloned.1.call-start = ((), (), s32[]{:S(2)}) async-start(), calls=%async_computation | async-start | bytes 3145728 | tf_op jit(solution)/shard_map/psum | solution.py:1784
Sparse Core Ops, SparseCore 0:
  202.1 133.7 all-reduce.1

commit v4 on v3

--- a/solution.py
+++ b/solution.py
@@ -1098,30 +1098,17 @@
     grad_down = grad_out.astype(low_type)
     vec_grad[9:10] += col_sum(grad_down)
     grad_source = jnp.zeros_like(total)
-    grad_turned, source_turned = grad_down.T, source.T
     for place in range(0, H, wide):
         span = slice(place, place + wide)
         grad_up = (slope[:, span] * nn(grad_down, weights[2, :, span])).astype(low_type)
         up_grad[:, span] += col_sum(grad_up)
         grad_source = grad_source + nt(grad_up, weights[1, :, span])
-        piece = nn(grad_turned, active[:, span])
-        other = nn(source_turned, grad_up)
+        piece = tn(grad_down, active[:, span])
+        other = tn(source, grad_up)
         for tile in range(wide // LANES):
             lane = slice(tile * LANES, (tile + 1) * LANES)
             acc_down[place // LANES + tile] += piece[:, lane]
             acc_up[place // LANES + tile] += other[:, lane]
-
-        @pl.when(step == last)
-        def _():
-            tiles = wide // LANES
-            tile, block = place // LANES, place // LANES // 2
-            rows_block = E // 4
-            for number, (acc, base) in enumerate(((acc_up, 2176), (acc_down, 2432))):
-                send_tiles(
-                    acc.at[pl.ds(tile, tiles)], blob.at[pl.ds(block, tiles // 2)], sems.at[number], tiles,
-                    rows_block, 2, base, rows_block,
-                )
-
     unit, rate = standard(middle[...])
     vec_grad[7:8] += col_sum(grad_source * unit)
     vec_grad[8:9] += col_sum(grad_source)
@@ -1137,6 +1124,8 @@
     @pl.when(step == last)
     def _():
         rows_block = E // 4
+        send_tiles(acc_up, blob, sems.at[0], H // LANES, rows_block, 2, 2176, rows_block)
+        send_tiles(acc_down, blob, sems.at[1], H // LANES, rows_block, 2, 2432, rows_block)
         send_tiles(acc_out, blob.at[pl.ds(6, 2)], sems.at[2], E // LANES, rows_block, 2, 1920, rows_block)
         wait_tiles(acc_up, sems.at[0])
         wait_tiles(acc_down, sems.at[1])
@@ -1170,9 +1159,9 @@
         grads[:, 2 * E + lane : 2 * E + lane + LANES] = value.astype(low_type)
     vec_grad[4:5] += col_sum(grads[:, :E])
     vec_grad[5:6] += col_sum(grads[:, 2 * E :])
-    rows = normed[...].T
+    rows = normed[...]
     for part in range(3):
-        piece = nn(rows, grads[:, part * E : (part + 1) * E])
+        piece = tn(rows, grads[:, part * E : (part + 1) * E])
         for tile in range(E // LANES):
             acc[part * (E // LANES) + tile] += piece[:, tile * LANES : (tile + 1) * LANES]
     grad_normed = nt(grads[...], weights[0, :, : 3 * E])
@@ -1193,7 +1182,7 @@
 
 def enc_ffn_back_kernel(last, blob_in, grad_entry, latent, output, middle, normed_two, slope, active, ffn, proj, vec,
                         grad_middle, vec_grad, up_grad, entry_grad, blob,
-                        grad_out, grad_down, grad_turned, source_turned, grad_source, folded, acc_up, acc_down, fold_sem, sems):
+                        grad_out, grad_down, grad_source, folded, acc_up, acc_down, fold_sem, sems):
     step = pl.program_id(0)
     fold_copy = pltpu.make_async_copy(folded, blob.at[:, :, pl.ds(2688, 96)], fold_sem)
     part_rows = D // 4
@@ -1219,8 +1208,6 @@
         rows = standard_back(unit, rate, grad_latent * vec[10:11])
         grad_out[...] = rows
         grad_down[...] = rows.astype(low_type)
-        grad_turned[...] = rows.T.astype(low_type)
-        source_turned[...] = normed_two[...].T
         vec_grad[9:10] = col_sum(rows.astype(low_type))
         grad_source[...] = jnp.zeros_like(grad_source)
 
@@ -1235,8 +1222,8 @@
     grad_up = (slope[...] * nn(grads, ffn[1])).astype(low_type)
     up_grad[...] = col_sum(grad_up)
     grad_source[...] += nt(grad_up, ffn[0])
-    piece = nn(grad_turned[...], active[...])
-    other = nn(source_turned[...], grad_up)
+    piece = tn(grads, active[...])
+    other = tn(normed_two[...], grad_up)
     count = grad_up.shape[1] // LANES
     for tile in range(count):
         lane = slice(tile * LANES, (tile + 1) * LANES)
@@ -1297,9 +1284,9 @@
         grads[:, 2 * D + lane : 2 * D + lane + LANES] = value.astype(low_type)
     vec_grad[4:5] = col_sum(grads[:, :D])
     vec_grad[5:6] = col_sum(grads[:, 2 * D :])
-    rows_in = normed[...].T
+    rows_in = normed[...]
     for part in range(3):
-        grad_wide[:, (part + 1) * D : (part + 2) * D] = nn(rows_in, grads[:, part * D : (part + 1) * D])
+        grad_wide[:, (part + 1) * D : (part + 2) * D] = tn(rows_in, grads[:, part * D : (part + 1) * D])
     width = 5 * D // 8
     tall = D // 4
 
@@ -1687,8 +1674,6 @@
         scratch_shapes=[
             vm((rows, D), high_type),
             vm((rows, D), low_type),
-            vm((D, rows), low_type),
-            vm((D, rows), low_type),
             vm((rows, D), high_type),
             vm((8, 4, 96, LANES), high_type),
             vm((2, chunk // LANES, D, LANES), high_type),

time: 418 us -> 415 us (level)
  transfers between devices with their start and end apart: 1 -> 1, of which waited for: 0 -> 0; matrix products, arithmetic and copies ran while one was open for 0% -> 0% of each run, Pallas kernels for 46% -> 47%
where the time goes in v4:
time: 415 us; the launch traced here: 407 us
  Pallas kernels  390 us (94%)
  between operations  14.3 us (3%)
    pallas_call x1, Pallas kernels, reduce_blocks(): pl.pallas_call(functools.partial(reduce_kernel, depth, devices, cols, par...  121 us
    pallas_call x1, Pallas kernels, gather_encode(): pl.pallas_call(functools.partial(gather_encode_kernel, depth, batch), out...  113 us
    pallas_call x1, Pallas kernels, local_grads(): pl.pallas_call(functools.partial(dec_ffn_kernel, images, batch // images...  46.7 us
    pallas_call x1, Pallas kernels, local_grads(): pl.pallas_call(functools.partial(dec_back_kernel, batch - 1), grid=(batch...  30.1 us
    pallas_call x1, Pallas kernels, local_grads(): pl.pallas_call(dec_attend_kernel, grid=(batch,), out_shape=(shape((dec_ro...  23.6 us
    pallas_call x1, Pallas kernels, local_grads(): pl.pallas_call(functools.partial(enc_ffn_back_kernel, F // chunk - 1), gr...  21.3 us
    pallas_call x1, Pallas kernels, local_grads(): pl.pallas_call(functools.partial(enc_back_kernel, batch), out_shape=(shap...  16.2 us
    pallas_call x1, Pallas kernels, apply_updates(): pl.pallas_call(functools.partial(adam_kernel, count), out_shape=tuple((sh...  10.8 us
  transfers between devices with their start and end apart: 1, of which 0 were waited for; matrix products, arithmetic and copies ran while one was open for 0% of the time, Pallas kernels for 47%

profile of v4, /device:TPU:0, one launch (start us, length us, event | category | flops | bytes accessed | tf_op | source)
XLA Modules:
  0.0 407.0 jit_solution(18216285415665565457)
XLA Ops:
  7.2 0.0 all-reduce.2.cloned.1.call-start
  7.2 4.5 %prepare.1 = (bf16[192,480]{1,0:T(8,128)(2,1)}, bf16[2,192,384]{2,1,0:T(8,128)(2,1)}, bf16[192,64]{1,0:T(8,128)(2,1)}, bf16[3,128,256]{2,1,0:T(8,128)(2,1)}, bf1...) custom-call(f32[192,480]{1,0:T(8,128)} %refs_3_.1, ...), custom_call_target="tpu_custom_call" | custom-call | tf_op jit(solution)/shard_map/prepare/pallas_call | solution.py:1400
  11.8 113.5 %gather_encode.1 = (bf16[2,768,3072]{2,1,0:T(8,128)(2,1)}, bf16[8,768,64]{2,1,0:T(8,128)(2,1)}, bf16[3,512,2048]{2,1,0:T(8,128)(2,1)}, bf16[768,3840]{1,0:T(8,12...) custom-call(bf16[192,480]{1,0:T(8,128)(2,1)} %get-tuple-element.98.o, ...), custom_call_target="tpu_custom_call" | custom-call | tf_op jit(solution)/shard_map/gather_encode/pallas_call | solution.py:465
  125.3 1.7 copy.51
  126.9 1.2 copy.52.proj
  128.2 23.6 %dec_attend.1 = (f32[1248,512]{1,0:T(8,128)}, bf16[1248,512]{1,0:T(8,128)(2,1)}, bf16[1248,1536]{1,0:T(8,128)(2,1)}, bf16[1248,512]{1,0:T(8,128)(2,1)}, f32[1248,512]{1,0:T(8,128)}, /*index=5*/bf16[1248,512]{1,0:T(8,128)(2,1)}) custom-call(bf16[384,768]{1,0:T(8,128)(2,1)} %get-tuple-element.106.latent, bf16[768,512]{1,0:T(8,128)(2,1)} %copy.52.proj, ...), custom_call_target="tpu_custom_call" | custom-call | tf_op jit(solution)/shard_map/dec_attend/pallas_call | solution.py:1538
  151.8 46.7 %dec_ffn.3 = (f32[1248,512]{1,0:T(8,128)}, bf16[1248,512]{1,0:T(8,128)(2,1)}, f32[512,768]{1,0:T(8,128)}, f32[12,512]{1,0:T(8,128)}, f32[1,2048]{1,0:T(1,128)}, ...) custom-call(f32[1248,512]{1,0:T(8,128)} %get-tuple-element.111.middle, ...), custom_call_target="tpu_custom_call" | custom-call | tf_op jit(solution)/shard_map/dec_ffn/pallas_call | solution.py:1574
  198.4 0.0 all-reduce.2.cloned.1.call-update
  198.5 30.1 %dec_back.1 = (bf16[384,512]{1,0:T(8,128)(2,1)}, f32[12,512]{1,0:T(8,128)}, f32[8,4,2784,128]{3,2,1,0:T(8,128)}) custom-call(f32[8,4,2784,128]{3,2,1,0:T(8,128)} %get-tuple-element.117.blob_in, bf16[1248,1536]{1,0:T(8,128)(2,1)} %get-tuple-element.118.qkv, bf16[1248,512]{1,0:T(8,128)(2,1)} %get-tuple-element.119.normed, ...), custom_call_target="tpu_custom_call", output_to_operand_aliasing={{2}: (0, {})} | custom-call | tf_op jit(solution)/shard_map/dec_back/pallas_call | solution.py:1621
  228.6 21.3 %enc_ffn_back.1 = (f32[384,768]{1,0:T(8,128)}, f32[12,768]{1,0:T(8,128)}, f32[1,3072]{1,0:T(1,128)}, f32[1,512]{1,0:T(1,128)}, f32[8,4,2784,128]{3,2,1,0:T(8,128)}) custom-call(f32[8,4,2784,128]{3,2,1,0:T(8,128)} %get-tuple-element.123.blob_in, bf16[384,512]{1,0:T(8,128)(2,1)} %get-tuple-element.124.grad_entry, ...), custom_call_target="tpu_custom_call", output_to_operand_aliasing={{4}: (0, {})} | custom-call | tf_op jit(solution)/shard_map/enc_ffn_back/pallas_call | solution.py:1644
  249.9 16.2 %enc_back.1 = (f32[12,768]{1,0:T(8,128)}, f32[8,4,2784,128]{3,2,1,0:T(8,128)}) custom-call(f32[8,4,2784,128]{3,2,1,0:T(8,128)} %get-tuple-element.131.blob_in, bf16[384,2304]{1,0:T(8,128)(2,1)} %get-tuple-element.132.qkv, bf16[384,768]{1,0:T(8,128)(2,1)} %get-tuple-element.133.kept, ...), custom_call_target="tpu_custom_call", output_to_operand_aliasing={{1}: (0, {})} | custom-call | tf_op jit(solution)/shard_map/enc_back/pallas_call | solution.py:1688
  266.1 1.6 pack.1
  267.7 121.4 %reduce_blocks.1 = (f32[2784,128]{1,0:T(8,128)}, f32[32,8,128]{2,1,0:T(8,128)}) custom-call(f32[8,4,2784,128]{3,2,1,0:T(8,128)} %get-tuple-element.139.blob, f32[32,8,128]{2,1,0:T(8,128)} %bitcast.21), custom_call_target="tpu_custom_call" | custom-call | tf_op jit(solution)/shard_map/reduce_blocks/pallas_call | solution.py:768
  389.1 0.0 all-reduce.2.cloned.1.call-done.refs_1_
  389.1 10.8 %adam.1 = (f32[192,480]{1,0:T(8,128)}, f32[2,192,384]{2,1,0:T(8,128)}, f32[64,192]{1,0:T(8,128)}, f32[128,256]{1,0:T(8,128)}, f32[2,128,256]{2,1,0:T(8,128)}, /*...) custom-call(f32[2784,128]{1,0:T(8,128)} %get-tuple-element.149.refs_, ...), custom_call_target="tpu_custom_call" | custom-call | tf_op jit(solution)/shard_map/adam/pallas_call | solution.py:1775
Async XLA Ops:
  7.2 381.9 %all-reduce.2.cloned.1.call-start = ((), (), s32[]{:S(2)}) async-start(), calls=%async_computation | async-start | bytes 3145728 | tf_op jit(solution)/shard_map/psum | solution.py:1769
Sparse Core Ops, SparseCore 0:
  198.6 133.7 all-reduce.1
